TPU v7x, 32 devices: a whole 2x2x4 slice. The times are simulated.
32 devices in a mesh: leaf: 8 (over z, y), front: 4 (over x, core).
Axes of the slice: x: 2, y: 2, z: 4, core: 2. Of those that a mesh axis runs over, the one named last changes fastest.
Arguments:
- child_u: bfloat16 [131072, 128], P(('leaf', 'front')), may hold values from -6 to 6
- child_v: bfloat16 [131072, 128], P(('leaf', 'front')), may hold values from -0.59765625 to 0.59765625
- sketch: bfloat16 [3, 131072, 128], P(None, ('leaf', 'front')), may hold values from -6 to 6
- map_own: int32 [3, 131072], P(None, ('leaf', 'front')), may hold values from 0 to 4095
- map_peer: int32 [3, 131072], P(None, ('leaf', 'front')), may hold values from 0 to 4095
- live_rows: int32 [3, 32], P(None, ('leaf', 'front')), may hold values from 1 to 4096, 81920 in all within a row
- front_panel: bfloat16 [131072, 128], P(('leaf', 'front')), may hold values from -6 to 6
- pivot_inverse: bfloat16 [1024, 128], P('leaf'), may hold values from -0.5 to 0.5
Outputs:
- left_out: bfloat16 [131072, 128], P(('leaf', 'front'))
- right_out: bfloat16 [131072, 128], P(('leaf', 'front'))
- panel_out: bfloat16 [131072, 128], P(('leaf', 'front'))
Inputs may be any that keep to these rules, and one draw needn't show every extreme that they name: `live_rows`: in each level every row of 32 counts sums to 81920, the largest being 4096 and the smallest at least 32.
All inputs are finite; a program needn't handle non-finite values. No bound on the sum of `live_rows` on one device may be relied on, other than what follows from the above.
Results may differ from a plain program's by a relative error of at most 0.01235.
Values may be sent and summed in bfloat16 or wider, within the bound.
A program may use at most 64 MiB of HBM per device.

v0:
```python
import math

import jax
import jax.numpy as jnp
from jax import lax
from jax.sharding import PartitionSpec as P

HIGHEST_PREC = lax.Precision.HIGHEST


def from_partner(block, axis, stride):
    count = lax.axis_size(axis)
    route = []
    for low in range(count):
        high = low | 1 << stride
        if high != low and high < count:
            route += [(low, high), (high, low)]
    return lax.ppermute(block, axis, route)


def broadcast(shard, axis, root):
    mine = lax.axis_index(axis) == root
    return lax.psum(jnp.where(mine, shard, jnp.zeros_like(shard)), axis)


def contract(first, second):
    return lax.dot_general(
        first,
        second,
        (((0,), (0,)), ((), ())),
        preferred_element_type=jnp.float32,
        precision=HIGHEST_PREC,
    )


def group_sum(partial_sum, tree_level):
    total = lax.psum(partial_sum, "front")
    for bit_index in range(tree_level + 1):
        total = total + from_partner(total, "leaf", bit_index)
    return total


def on_device(child_u, child_v, sketch, map_own, map_peer, live_rows, front_panel, pivot_inverse):
    row_count = child_u.shape[0]
    level_count = sketch.shape[0]
    panel_width = pivot_inverse.shape[0]
    front_count = lax.axis_size("front")
    left = child_u
    right = child_v
    for tree_level in range(level_count):
        sibling = from_partner(jnp.stack([left, right]), "leaf", tree_level)
        row_keep = (jnp.arange(row_count, dtype=jnp.int32) < live_rows[tree_level, 0])[:, None]
        map_self = map_own[tree_level]
        map_other = map_peer[tree_level]
        left_cat = jnp.where(
            row_keep, jnp.concatenate([left[map_self], sibling[0][map_other]], 1), 0
        )
        right_cat = jnp.where(
            row_keep, jnp.concatenate([right[map_self], sibling[1][map_other]], 1), 0
        )
        left_wide = left_cat.astype(jnp.float32)
        right_wide = right_cat.astype(jnp.float32)
        sketch_part = contract(right_wide, sketch[tree_level].astype(jnp.float32))
        norm_scale = math.sqrt(2 ** (tree_level + 1) * front_count * row_count)
        sketch_b = group_sum(sketch_part, tree_level)
        basis = jnp.dot(left_wide, sketch_b, precision=HIGHEST_PREC)
        gram = group_sum(contract(basis, basis), tree_level)
        lower = jnp.linalg.cholesky(gram)
        ortho = lax.linalg.triangular_solve(
            lower, basis, left_side=False, lower=True, transpose_a=True
        )
        project = group_sum(contract(left_wide, ortho), tree_level)
        left = (ortho * norm_scale).astype(jnp.bfloat16)
        right = (jnp.dot(right_wide, project, precision=HIGHEST_PREC) / norm_scale).astype(
            jnp.bfloat16
        )
    right_piv = broadcast(right[:panel_width], "front", 0)
    updated = front_panel.astype(jnp.float32) - lax.dot_general(
        left, right_piv, (((1,), (1,)), ((), ())), preferred_element_type=jnp.float32
    )
    panel_out = jnp.dot(updated, pivot_inverse.astype(jnp.float32), precision=HIGHEST_PREC).astype(
        jnp.bfloat16
    )
    return (left, right, panel_out)


def solution(mesh):
    placed = (
        P(("leaf", "front"), None),
        P(("leaf", "front"), None),
        P(None, ("leaf", "front"), None),
        P(None, ("leaf", "front")),
        P(None, ("leaf", "front")),
        P(None, ("leaf", "front")),
        P(("leaf", "front"), None),
        P("leaf", None),
    )
    return jax.shard_map(
        on_device,
        mesh=mesh,
        in_specs=placed,
        out_specs=(
            P(("leaf", "front"), None),
            P(("leaf", "front"), None),
            P(("leaf", "front"), None),
        ),
        check_vma=False,
    )
```

profile of v0, /device:TPU:25, one launch (start us, length us, event | category | flops | bytes accessed | tf_op | source)
XLA Modules:
  0.0 866.2 jit_solution(9598980988570298098)
XLA Ops:
  10.5 15.0 %gather_fusion.2 = bf16[4096,128]{1,0:T(8,128)(2,1)} fusion(bf16[4096,128]{1,0:T(8,128)(2,1)S(1)} %copy-done.1, s32[4096]{0:T(1024)S(1)} %broadcast_clamp_fusion.5), kind=kCustom, calls=%fused_computation.2 | custom fusion | bytes 2113536 | tf_op jit(solution)/shard_map/gather | solution.py:59
  26.9 28.8 %collective-permute-done = bf16[2,4096,128]{2,1,0:T(8,128)(2,1)} collective-permute-done((bf16[2,4096,128]{2,1,0:T(8,128)(2,1)S(1)}, bf16[2,4096,128]{2,1,0:T(8,128)(2,1)}, u32[]{:S(2)}, u32[]{:S(2)}) %collective-permute-start) | collective-permute-done | bytes 2097184 | tf_op jit(solution)/shard_map/ppermute | solution.py:18
  57.4 15.0 %gather_fusion.3 = bf16[4096,128]{1,0:T(8,128)(2,1)} fusion(bf16[4096,128]{1,0:T(8,128)(2,1)S(1)} %get-tuple-element.16, s32[4096]{0:T(1024)S(1)} %broadcast_clamp_fusion.4), kind=kCustom, calls=%fused_computation.3 | custom fusion | bytes 2113536 | tf_op jit(solution)/shard_map/gather | solution.py:59
  72.5 3.7 fusion.7
  76.2 32.3 %all-reduce.10.cloned.1.call-done = f32[256,128]{1,0:T(8,128)} async-done(((f32[256,128]{1,0:T(8,128)}), f32[256,128]{1,0:T(8,128)}) %all-reduce.10.cloned.1.call-update) | async-done | bytes 131088 | tf_op jit(solution)/shard_map/psum | solution.py:37
  109.7 15.0 %gather_fusion = bf16[4096,128]{1,0:T(8,128)(2,1)} fusion(bf16[4096,128]{1,0:T(8,128)(2,1)S(1)} %copy-done.2, s32[4096]{0:T(1024)S(1)} %broadcast_clamp_fusion.5), kind=kCustom, calls=%fused_computation | custom fusion | bytes 2113536 | tf_op jit(solution)/shard_map/gather | solution.py:56
  124.7 15.0 %gather_fusion.1 = bf16[4096,128]{1,0:T(8,128)(2,1)} fusion(bf16[4096,128]{1,0:T(8,128)(2,1)S(1)} %get-tuple-element.15, s32[4096]{0:T(1024)S(1)} %broadcast_clamp_fusion.4), kind=kCustom, calls=%fused_computation.1 | custom fusion | bytes 2113536 | tf_op jit(solution)/shard_map/gather | solution.py:56
  139.8 4.1 fusion.19
  143.8 4.1 fusion.62
  148.2 30.3 %all-reduce.12.cloned.1.call-done = f32[128,128]{0,1:T(8,128)} async-done(((f32[128,128]{0,1:T(8,128)}), f32[128,128]{0,1:T(8,128)}) %all-reduce.12.cloned.1.call-update) | async-done | bytes 65552 | tf_op jit(solution)/shard_map/psum | solution.py:37
  182.8 11.7 %cholesky.59 = f32[128,128]{1,0:T(8,128)S(1)} custom-call(f32[128,128]{1,0:T(8,128)S(1)} %fusion.32), custom_call_target="Cholesky" | custom-call | tf_op jit(solution)/shard_map/jit(cholesky)/cholesky | solution.py:68
  195.9 9.8 %custom-call.7 = f32[1,128,128]{1,2,0:T(8,128)S(1)} custom-call(f32[1,128,128]{2,1,0:T(8,128)S(1)} %fusion.24), custom_call_target="InvertDiagBlocksLowerTriangular" | custom-call | tf_op jit(solution)/shard_map/triangular_solve/custom-call.0 | solution.py:69
  207.8 3.7 fusion.23
  212.0 32.2 %all-reduce.14.cloned.1.call-done = f32[256,128]{1,0:T(8,128)} async-done(((f32[256,128]{1,0:T(8,128)}), f32[256,128]{1,0:T(8,128)}) %all-reduce.14.cloned.1.call-update) | async-done | bytes 131088 | tf_op jit(solution)/shard_map/psum | solution.py:37
  248.2 3.7 fusion
  255.1 15.0 %gather_fusion.6 = bf16[4096,128]{1,0:T(8,128)(2,1)} fusion(bf16[4096,128]{1,0:T(8,128)(2,1)S(1)} %copy.33, s32[4096]{0:T(1024)S(1)} %broadcast_clamp_fusion.3), kind=kCustom, calls=%fused_computation.6 | custom fusion | bytes 2113536 | tf_op jit(solution)/shard_map/gather | solution.py:59
  270.1 27.9 %collective-permute-done.4 = bf16[2,4096,128]{1,2,0:T(8,128)(2,1)} collective-permute-done((bf16[2,4096,128]{1,2,0:T(8,128)(2,1)}, bf16[2,4096,128]{1,2,0:T(8,128)(2,1)}, u32[]{:S(2)}, u32[]{:S(2)}) %collective-permute-start.4) | collective-permute-done | bytes 2097184 | tf_op jit(solution)/shard_map/ppermute | solution.py:18
  302.4 15.0 %gather_fusion.7 = bf16[4096,128]{1,0:T(8,128)(2,1)} fusion(bf16[4096,128]{1,0:T(8,128)(2,1)S(1)} %copy.34, s32[4096]{0:T(1024)S(1)} %broadcast_clamp_fusion.2), kind=kCustom, calls=%fused_computation.7 | custom fusion | bytes 2113536 | tf_op jit(solution)/shard_map/gather | solution.py:59
  317.4 3.7 fusion.5
  321.1 33.8 %all-reduce.16.cloned.1.call-done = f32[256,128]{1,0:T(8,128)} async-done(((f32[256,128]{1,0:T(8,128)}), f32[256,128]{1,0:T(8,128)}) %all-reduce.16.cloned.1.call-update) | async-done | bytes 131088 | tf_op jit(solution)/shard_map/psum | solution.py:37
  360.9 15.0 %gather_fusion.4 = bf16[4096,128]{1,0:T(8,128)(2,1)} fusion(bf16[4096,128]{1,0:T(8,128)(2,1)S(1)} %copy.30, s32[4096]{0:T(1024)S(1)} %broadcast_clamp_fusion.3), kind=kCustom, calls=%fused_computation.4 | custom fusion | bytes 2113536 | tf_op jit(solution)/shard_map/gather | solution.py:56
  376.6 15.0 %gather_fusion.5 = bf16[4096,128]{1,0:T(8,128)(2,1)} fusion(bf16[4096,128]{1,0:T(8,128)(2,1)S(1)} %copy.32, s32[4096]{0:T(1024)S(1)} %broadcast_clamp_fusion.2), kind=kCustom, calls=%fused_computation.5 | custom fusion | bytes 2113536 | tf_op jit(solution)/shard_map/gather | solution.py:56
  391.6 4.0 fusion.16
  395.6 4.1 fusion.63
  400.0 32.5 %all-reduce.18.cloned.1.call-done = f32[128,128]{0,1:T(8,128)} async-done(((f32[128,128]{0,1:T(8,128)}), f32[128,128]{0,1:T(8,128)}) %all-reduce.18.cloned.1.call-update) | async-done | bytes 65552 | tf_op jit(solution)/shard_map/psum | solution.py:37
  439.9 11.7 %cholesky.70 = f32[128,128]{1,0:T(8,128)S(1)} custom-call(f32[128,128]{1,0:T(8,128)S(1)} %fusion.30), custom_call_target="Cholesky" | custom-call | tf_op jit(solution)/shard_map/jit(cholesky)/cholesky | solution.py:68
  453.0 9.8 %custom-call.8 = f32[1,128,128]{1,2,0:T(8,128)S(1)} custom-call(f32[1,128,128]{2,1,0:T(8,128)S(1)} %fusion.25), custom_call_target="InvertDiagBlocksLowerTriangular" | custom-call | tf_op jit(solution)/shard_map/triangular_solve/custom-call.0 | solution.py:69
  464.8 3.7 fusion.22
  468.8 33.6 %all-reduce.20.cloned.1.call-done = f32[256,128]{1,0:T(8,128)} async-done(((f32[256,128]{1,0:T(8,128)}), f32[256,128]{1,0:T(8,128)}) %all-reduce.20.cloned.1.call-update) | async-done | bytes 131088 | tf_op jit(solution)/shard_map/psum | solution.py:37
  511.3 3.7 fusion.1
  518.1 15.0 %gather_fusion.10 = bf16[4096,128]{1,0:T(8,128)(2,1)} fusion(bf16[4096,128]{1,0:T(8,128)(2,1)S(1)} %copy.40, s32[4096]{0:T(1024)S(1)} %broadcast_clamp_fusion.1), kind=kCustom, calls=%fused_computation.10 | custom fusion | bytes 2113536 | tf_op jit(solution)/shard_map/gather | solution.py:59
  533.1 77.1 %collective-permute-done.11 = bf16[2,4096,128]{1,2,0:T(8,128)(2,1)} collective-permute-done((bf16[2,4096,128]{1,2,0:T(8,128)(2,1)}, bf16[2,4096,128]{1,2,0:T(8,128)(2,1)}, u32[]{:S(2)}, u32[]{:S(2)}) %collective-permute-start.11) | collective-permute-done | bytes 2097184 | tf_op jit(solution)/shard_map/ppermute | solution.py:18
  614.5 15.0 %gather_fusion.11 = bf16[4096,128]{1,0:T(8,128)(2,1)} fusion(bf16[4096,128]{1,0:T(8,128)(2,1)S(1)} %copy.41, s32[4096]{0:T(1024)S(1)} %broadcast_clamp_fusion), kind=kCustom, calls=%fused_computation.11 | custom fusion | bytes 2113536 | tf_op jit(solution)/shard_map/gather | solution.py:59
  629.5 3.7 fusion.3
  633.2 30.6 %all-reduce.22.cloned.1.call-done = f32[256,128]{1,0:T(8,128)} async-done(((f32[256,128]{1,0:T(8,128)}), f32[256,128]{1,0:T(8,128)}) %all-reduce.22.cloned.1.call-update) | async-done | bytes 131088 | tf_op jit(solution)/shard_map/psum | solution.py:37
  673.6 15.0 %gather_fusion.8 = bf16[4096,128]{1,0:T(8,128)(2,1)} fusion(bf16[4096,128]{1,0:T(8,128)(2,1)S(1)} %copy.37, s32[4096]{0:T(1024)S(1)} %broadcast_clamp_fusion.1), kind=kCustom, calls=%fused_computation.8 | custom fusion | bytes 2113536 | tf_op jit(solution)/shard_map/gather | solution.py:56
  689.3 15.0 %gather_fusion.9 = bf16[4096,128]{1,0:T(8,128)(2,1)} fusion(bf16[4096,128]{1,0:T(8,128)(2,1)S(1)} %copy.39, s32[4096]{0:T(1024)S(1)} %broadcast_clamp_fusion), kind=kCustom, calls=%fused_computation.9 | custom fusion | bytes 2113536 | tf_op jit(solution)/shard_map/gather | solution.py:56
  704.3 4.0 fusion.13
  708.3 4.1 fusion.64
  712.7 33.5 %all-reduce.24.cloned.1.call-done = f32[128,128]{0,1:T(8,128)} async-done(((f32[128,128]{0,1:T(8,128)}), f32[128,128]{0,1:T(8,128)}) %all-reduce.24.cloned.1.call-update) | async-done | bytes 65552 | tf_op jit(solution)/shard_map/psum | solution.py:37
  753.9 4.5 collective-permute-done.17
  758.5 11.7 %cholesky.81 = f32[128,128]{1,0:T(8,128)S(1)} custom-call(f32[128,128]{1,0:T(8,128)S(1)} %fusion.28), custom_call_target="Cholesky" | custom-call | tf_op jit(solution)/shard_map/jit(cholesky)/cholesky | solution.py:68
  771.6 9.8 %custom-call.9 = f32[1,128,128]{1,2,0:T(8,128)S(1)} custom-call(f32[1,128,128]{2,1,0:T(8,128)S(1)} %fusion.26), custom_call_target="InvertDiagBlocksLowerTriangular" | custom-call | tf_op jit(solution)/shard_map/triangular_solve/custom-call.0 | solution.py:69
  783.5 3.7 fusion.21
  787.2 35.0 %all-reduce.26.cloned.1.call-done = f32[256,128]{1,0:T(8,128)} async-done(((f32[256,128]{1,0:T(8,128)}), f32[256,128]{1,0:T(8,128)}) %all-reduce.26.cloned.1.call-update) | async-done | bytes 131088 | tf_op jit(solution)/shard_map/psum | solution.py:37
  827.5 3.6 collective-permute-done.19
  833.0 4.3 collective-permute-done.20
  840.7 14.6 %psum.79 = bf16[128,128]{1,0:T(8,128)(2,1)S(1)} all-reduce(bf16[128,128]{1,0:T(8,128)(2,1)S(1)} %slice_select_fusion), channel_id=1, replica_groups=mesh['leaf'=8,'front'=4] {'front'}, use_global_device_ids=true, to_apply=%region_11.14 | all-reduce | flops 16384 | bytes 65536 | tf_op jit(solution)/shard_map/psum | solution.py:23
  (153 shorter events, 98.0 us)
Async XLA Ops:
  7.2 849.9 %copy-start = (bf16[128,128]{1,0:T(8,128)(2,1)S(1)}, bf16[128,128]{1,0:T(8,128)(2,1)}, u32[]{:S(2)}) copy-start(bf16[128,128]{1,0:T(8,128)(2,1)} %param.18) | copy-start | bytes 98308
  7.2 101.4 %all-reduce.10.cloned.1.call-start = ((), (), s32[]{:S(2)}) async-start(), calls=%async_computation | async-start | bytes 262144 | tf_op jit(solution)/shard_map/psum | solution.py:37
  7.2 3.2 copy-start.14
  7.2 3.2 copy-start.1
  9.1 46.7 %collective-permute-start = (bf16[2,4096,128]{2,1,0:T(8,128)(2,1)S(1)}, bf16[2,4096,128]{2,1,0:T(8,128)(2,1)}, u32[]{:S(2)}, u32[]{:S(2)}) collective-permute-start(bf16[2,4096,128]{2,1,0:T(8,128)(2,1)S(1)} %pad_maximum_fusion), channel_id=1, source_target_pairs={{0,4},{4,0},{8,12},{12,8},{16,20},{20,16},{24,28},{28,24},{1,5},{5... | collective-permute-start | bytes 6291464 | tf_op jit(solution)/shard_map/ppermute | solution.py:18
  10.5 15.1 %copy-start.16 = (s32[3,1]{0,1:T(1,128)S(1)}, s32[3,1]{0,1:T(1,128)}, u32[]{:S(2)}) copy-start(s32[3,1]{0,1:T(1,128)} %param.16) | copy-start | bytes 40
  10.5 16.4 %copy-start.15 = (s32[3,4096]{1,0:T(4,128)S(1)}, s32[3,4096]{1,0:T(4,128)}, u32[]{:S(2)}) copy-start(s32[3,4096]{1,0:T(4,128)} %param.15) | copy-start | bytes 147460
  57.4 15.0 %copy-start.6 = (bf16[4096,128]{1,0:T(8,128)(2,1)S(1)}, bf16[4096,128]{1,0:T(8,128)(2,1)}, u32[]{:S(2)}) copy-start(bf16[4096,128]{1,0:T(8,128)(2,1)} %gather_fusion.2) | copy-start | bytes 3145732
  72.5 37.3 %copy-start.2 = (bf16[4096,128]{1,0:T(8,128)(2,1)S(1)}, bf16[4096,128]{1,0:T(8,128)(2,1)}, u32[]{:S(2)}) copy-start(bf16[4096,128]{1,0:T(8,128)(2,1)} %param.11) | copy-start | bytes 3145732
  76.2 102.4 %all-reduce.12.cloned.1.call-start = ((), (), s32[]{:S(2)}) async-start(), calls=%async_computation.1 | async-start | bytes 131072 | tf_op jit(solution)/shard_map/psum | solution.py:37
  108.5 31.2 %collective-permute-start.1 = (f32[256,128]{1,0:T(8,128)}, f32[256,128]{1,0:T(8,128)}, u32[]{:S(2)}, u32[]{:S(2)}) collective-permute-start(f32[256,128]{1,0:T(8,128)} %all-reduce.10.cloned.1.call-done), channel_id=1, source_target_pairs={{0,4},{4,0},{8,12},{12,8},{16,20},{20,16},{24,28},{28,24},{1,5},{5... | collective-permute-start | bytes 393224 | tf_op jit(solution)/shard_map/ppermute | solution.py:18
  124.7 15.0 %copy-start.18 = (f32[256,128]{1,0:T(8,128)S(1)}, f32[256,128]{1,0:T(8,128)}, u32[]{:S(2)}) copy-start(f32[256,128]{1,0:T(8,128)} %all-reduce.10.cloned.1.call-done) | copy-start | bytes 393220
  147.9 96.3 %all-reduce.14.cloned.1.call-start = ((), (), s32[]{:S(2)}) async-start(), calls=%async_computation.2 | async-start | bytes 262144 | tf_op jit(solution)/shard_map/psum | solution.py:37
  178.5 3.3 collective-permute-start.2
  205.7 2.0 copy-start.12
  205.7 2.0 copy-start.13
  207.8 40.5 %copy-start.7 = (bf16[4096,128]{1,0:T(8,128)(2,1)S(1)}, bf16[4096,128]{1,0:T(8,128)(2,1)}, u32[]{:S(2)}) copy-start(bf16[4096,128]{1,0:T(8,128)(2,1)} %gather_fusion.2) | copy-start | bytes 3145732
  211.5 143.5 %all-reduce.16.cloned.1.call-start = ((), (), s32[]{:S(2)}) async-start(), calls=%async_computation.3 | async-start | bytes 262144 | tf_op jit(solution)/shard_map/psum | solution.py:37
  244.2 4.0 collective-permute-start.3
  253.5 44.6 %collective-permute-start.4 = (bf16[2,4096,128]{1,2,0:T(8,128)(2,1)}, bf16[2,4096,128]{1,2,0:T(8,128)(2,1)}, u32[]{:S(2)}, u32[]{:S(2)}) collective-permute-start(bf16[2,4096,128]{1,2,0:T(8,128)(2,1)} %pad_maximum_fusion.1), channel_id=1, source_target_pairs={{0,8},{8,0},{4,12},{12,4},{16,24},{24,16},{20,28},{28,20},{1,9},{9... | collective-permute-start | bytes 6291464 | tf_op jit(solution)/shard_map/ppermute | solution.py:18
  321.1 111.3 %all-reduce.18.cloned.1.call-start = ((), (), s32[]{:S(2)}) async-start(), calls=%async_computation.4 | async-start | bytes 131072 | tf_op jit(solution)/shard_map/psum | solution.py:37
  355.0 4.0 collective-permute-start.5
  359.9 31.7 %collective-permute-start.6 = (f32[256,128]{1,0:T(8,128)S(1)}, f32[256,128]{1,0:T(8,128)S(1)}, u32[]{:S(2)}, u32[]{:S(2)}) collective-permute-start(f32[256,128]{1,0:T(8,128)S(1)} %add.155), channel_id=1, source_target_pairs={{0,8},{8,0},{4,12},{12,4},{16,24},{24,16},{20,28},{28,20},{1,9},{9... | collective-permute-start | bytes 393224 | tf_op jit(solution)/shard_map/ppermute | solution.py:18
  399.7 102.7 %all-reduce.20.cloned.1.call-start = ((), (), s32[]{:S(2)}) async-start(), calls=%async_computation.5 | async-start | bytes 262144 | tf_op jit(solution)/shard_map/psum | solution.py:37
  432.4 3.3 collective-permute-start.7
  436.6 3.2 collective-permute-start.8
  462.8 2.0 copy-start.10
  462.8 2.0 copy-start.11
  464.8 46.4 %copy-start.5 = (bf16[4096,128]{1,0:T(8,128)(2,1)S(1)}, bf16[4096,128]{1,0:T(8,128)(2,1)}, u32[]{:S(2)}) copy-start(bf16[4096,128]{1,0:T(8,128)(2,1)} %gather_fusion.6) | copy-start | bytes 3145732
  468.6 195.2 %all-reduce.22.cloned.1.call-start = ((), (), s32[]{:S(2)}) async-start(), calls=%async_computation.6 | async-start | bytes 262144 | tf_op jit(solution)/shard_map/psum | solution.py:37
  502.4 4.0 collective-permute-start.9
  507.4 3.9 collective-permute-start.10
  516.5 93.7 %collective-permute-start.11 = (bf16[2,4096,128]{1,2,0:T(8,128)(2,1)}, bf16[2,4096,128]{1,2,0:T(8,128)(2,1)}, u32[]{:S(2)}, u32[]{:S(2)}) collective-permute-start(bf16[2,4096,128]{1,2,0:T(8,128)(2,1)} %pad_maximum_fusion.2), channel_id=1, source_target_pairs={{0,16},{16,0},{4,20},{20,4},{8,24},{24,8},{12,28},{28,12},{1,17},{... | collective-permute-start | bytes 6291464 | tf_op jit(solution)/shard_map/ppermute | solution.py:18
  633.2 113.1 %all-reduce.24.cloned.1.call-start = ((), (), s32[]{:S(2)}) async-start(), calls=%async_computation.7 | async-start | bytes 131072 | tf_op jit(solution)/shard_map/psum | solution.py:37
  663.8 4.0 collective-permute-start.12
  668.7 3.9 collective-permute-start.13
  672.6 31.7 %collective-permute-start.14 = (f32[256,128]{1,0:T(8,128)S(1)}, f32[256,128]{1,0:T(8,128)S(1)}, u32[]{:S(2)}, u32[]{:S(2)}) collective-permute-start(f32[256,128]{1,0:T(8,128)S(1)} %add.164), channel_id=1, source_target_pairs={{0,16},{16,0},{4,20},{20,4},{8,24},{24,8},{12,28},{28,12},{1,17},{... | collective-permute-start | bytes 393224 | tf_op jit(solution)/shard_map/ppermute | solution.py:18
  712.4 109.8 %all-reduce.26.cloned.1.call-start = ((), (), s32[]{:S(2)}) async-start(), calls=%async_computation.8 | async-start | bytes 262144 | tf_op jit(solution)/shard_map/psum | solution.py:37
  746.3 3.3 collective-permute-start.15
  750.4 3.2 collective-permute-start.16
  753.6 4.8 collective-permute-start.17
  781.4 2.1 copy-start.8
  781.4 2.1 copy-start.9
  787.2 50.1 %copy-start.3 = (bf16[4096,128]{1,0:T(8,128)(2,1)S(1)}, bf16[4096,128]{1,0:T(8,128)(2,1)}, u32[]{:S(2)}) copy-start(bf16[4096,128]{1,0:T(8,128)(2,1)} %gather_fusion.10) | copy-start | bytes 3145732
  787.2 50.1 %copy-start.4 = (bf16[4096,128]{1,0:T(8,128)(2,1)S(1)}, bf16[4096,128]{1,0:T(8,128)(2,1)}, u32[]{:S(2)}) copy-start(bf16[4096,128]{1,0:T(8,128)(2,1)} %gather_fusion.11) | copy-start | bytes 3145732
  822.2 4.0 collective-permute-start.18
  827.2 3.9 collective-permute-start.19
  831.1 6.2 collective-permute-start.20
  (1 other events, 1.0 us)
Sparse Core Ops, SparseCore 0:
  76.3 32.2 all-reduce.9
  148.0 30.4 all-reduce.11
  211.6 32.5 all-reduce.13
  321.2 33.7 all-reduce.15
  399.9 32.5 all-reduce.17
  468.7 33.6 all-reduce.19
  633.3 30.4 all-reduce.21
  712.6 33.6 all-reduce.23
  787.3 34.8 all-reduce.25
where the time goes:
time: 875 us; the launch traced here: 866 us
  waiting for transfers between devices  474 us (54%)
  local copies, waits for them, and re-layouts  198 us (23%)
  other arithmetic  82 us (9%)
  matrix products  66 us (8%)
  starting transfers between devices  17 us (2%)
  between operations  14.9 us (2%)
  blocking collectives  14.6 us (2%)
    psum x9, waiting for transfers between devices, group_sum(): total = lax.psum(partial_sum, 'front')  294 us
    ppermute x21, waiting for transfers between devices, from_partner(): return lax.ppermute(block, axis, route)  179 us
    gather x3, local copies, waits for them, and re-layouts, on_device(): sibling[1][map_other]  45.1 us
    gather x3, local copies, waits for them, and re-layouts, on_device(): right[map_self]  45.1 us
    gather x3, local copies, waits for them, and re-layouts, on_device(): sibling[0][map_other]  45.1 us
    gather x3, local copies, waits for them, and re-layouts, on_device(): left[map_self]  45 us
    another operation x9, other arithmetic, on_device(): lower = jnp.linalg.cholesky(gram)  37.2 us
    dot_general x9, matrix products, contract(): lax.dot_general(first, second, (((0,), (0,)), ((), ())), preferred_elemen...  34.3 us
  transfers between devices with their start and end apart: 30, of which 27 were waited for; matrix products, arithmetic and copies ran while one was open for 17% of the time, Pallas kernels for 0%

commit v1 on v0

v1 whole, which is shorter than its diff:
```python
import functools
import math

import jax
import jax.numpy as jnp
from jax import lax
from jax.experimental import pallas as pl
from jax.experimental.pallas import tpu as pltpu
from jax.sharding import PartitionSpec as P

BF16 = jnp.bfloat16
F32 = jnp.float32
HIGHEST_PREC = lax.Precision.HIGHEST
MESH = pl.DeviceIdType.MESH
VMEM_LIMIT = 48 * 1024 * 1024
UNROLL = 32
PIECE = 512

VMEM_SPEC = pl.BlockSpec(memory_space=pltpu.VMEM)
SMEM_SPEC = pl.BlockSpec(memory_space=pltpu.SMEM)


def from_partner(block, axis, stride):
    count = lax.axis_size(axis)
    route = []
    for low in range(count):
        high = low | 1 << stride
        if high != low and high < count:
            route += [(low, high), (high, low)]
    return lax.ppermute(block, axis, route)


def dot(first, second, dims=((1,), (0,)), precision=None):
    return lax.dot_general(
        first, second, (dims, ((), ())), preferred_element_type=F32, precision=precision
    )


def halves(wide):
    high = wide.astype(BF16)
    return high, (wide - high.astype(F32)).astype(BF16)


def gather_pairs(left_ref, right_ref, index_ref, live, table, picked):
    rows, width = left_ref.shape

    def fill(step, _):
        at = pl.multiple_of(step * PIECE, PIECE)
        table[pl.ds(2 * at, PIECE, stride=2), :] = left_ref[pl.ds(at, PIECE), :].astype(F32)
        table[pl.ds(2 * at + 1, PIECE, stride=2), :] = right_ref[pl.ds(at, PIECE), :].astype(F32)
        return 0

    lax.fori_loop(0, rows // PIECE, fill, 0)

    def pick(step, _):
        base = step * UNROLL
        loaded = []
        for j in range(UNROLL):
            loaded.append(table[pl.ds(2 * index_ref[base + j], 2), :])
        for j in range(UNROLL):
            picked[pl.ds(2 * (base + j), 2), :] = loaded[j]
        return 0

    lax.fori_loop(0, (live + UNROLL - 1) // UNROLL, pick, 0)


def read_pairs(picked, at, keep):
    first = picked[pl.ds(2 * at, PIECE, stride=2), :]
    second = picked[pl.ds(2 * at + 1, PIECE, stride=2), :]
    return jnp.where(keep, first, 0.0).astype(BF16), jnp.where(keep, second, 0.0).astype(BF16)


def keep_rows(at, live, width):
    return lax.broadcasted_iota(jnp.int32, (PIECE, width), 0) + at < live


def own_kernel(index_ref, live_ref, left_ref, right_ref, left_own, right_own, table, picked):
    rows, width = left_ref.shape
    live = live_ref[0, 0]
    gather_pairs(left_ref, right_ref, index_ref, live, table, picked)

    def store(step, _):
        at = pl.multiple_of(step * PIECE, PIECE)
        first, second = read_pairs(picked, at, keep_rows(at, live, width))
        left_own[pl.ds(at, PIECE), :] = first
        right_own[pl.ds(at, PIECE), :] = second
        return 0

    lax.fori_loop(0, rows // PIECE, store, 0)


def peer_kernel(
    index_ref, live_ref, left_ref, right_ref, left_own, right_own, sketch_ref,
    left_cat, right_cat, sums, table, picked,
):
    rows, width = left_ref.shape
    live = live_ref[0, 0]
    gather_pairs(left_ref, right_ref, index_ref, live, table, picked)
    sums[...] = jnp.zeros_like(sums)

    def add(step, _):
        at = pl.multiple_of(step * PIECE, PIECE)
        here = pl.ds(at, PIECE)
        first, second = read_pairs(picked, at, keep_rows(at, live, width))
        left_cat[here, :width] = left_own[here, :]
        left_cat[here, width:] = first
        right_cat[here, :width] = right_own[here, :]
        right_cat[here, width:] = second
        both = left_cat[here, :]
        gram = dot(both, both, ((0,), (0,)))
        sketched = dot(right_cat[here, :], sketch_ref[here, :], ((0,), (0,)))
        sums[: 2 * width, :] += sketched
        sums[2 * width : 3 * width, :] += gram[:width, :width]
        sums[3 * width : 4 * width, :] += gram[:width, width:]
        sums[4 * width : 5 * width, :] += gram[width:, width:]
        return 0

    lax.fori_loop(0, rows // PIECE, add, 0)


def inverse_factor(gram):
    size = gram.shape[0]
    tiles = [gram[8 * t : 8 * t + 8, :] for t in range(size // 8)]
    lane = lax.broadcasted_iota(jnp.int32, (8, size), 1)
    sublane = lax.broadcasted_iota(jnp.int32, (8, size), 0)
    pivots = [jnp.ones((8, size), F32) for _ in tiles]
    for k in range(size):
        own, within = divmod(k, 8)
        row = tiles[own][within : within + 1, :]
        pivot = row[:, k : k + 1]
        pivots[own] = jnp.where(sublane == within, pivot, pivots[own])
        scaled = row / pivot
        scaled = jnp.where(lane[:1] == k, 1.0 / pivot, scaled)
        for t in range(own, size // 8):
            column = tiles[t][:, k : k + 1]
            old = jnp.where(lane == k, 0.0, tiles[t])
            new = old - column * scaled
            if t == own:
                new = jnp.where(sublane > within, new, tiles[t])
                new = jnp.where((sublane == within) & (lane == k), 1.0, new)
            tiles[t] = new
    wide = [
        jnp.where(lane <= sublane + 8 * t, tile, 0.0) * lax.rsqrt(pivots[t])
        for t, tile in enumerate(tiles)
    ]
    return jnp.concatenate(wide, axis=0)


def front_kernel(
    level, pivot_rows, leaf_count, front_count,
    sums, left_cat, right_cat, *refs,
):
    last = pivot_rows > 0
    if last:
        panel, inverse, left_out, right_out, panel_out = refs[:5]
        parts, piece, total, pivots, send1, recv1, send2, recv2, send3, recv3 = refs[5:]
    else:
        left_out, right_out = refs[:2]
        parts, piece, total, send1, recv1, send2, recv2 = refs[2:]
    rows = left_cat.shape[0]
    width = left_cat.shape[1] // 2
    subtrees = 2 ** (level + 1)
    members = subtrees * front_count
    chunk = piece.shape[0]
    leaf, front = lax.axis_index("leaf"), lax.axis_index("front")
    low = lax.rem(leaf, subtrees)
    rank = low * front_count + front

    def device(place):
        return (leaf - low + place // front_count, lax.rem(place, front_count))

    barrier = pltpu.get_barrier_semaphore()

    def greet(d, _):
        pl.semaphore_signal(
            barrier, inc=1, device_id=device(lax.rem(rank + d, members)), device_id_type=MESH
        )
        return 0

    lax.fori_loop(1, members, greet, 0)
    pl.semaphore_wait(barrier, members - 1)

    def scatter(d):
        to = lax.rem(rank + d, members)
        return pltpu.make_async_remote_copy(
            src_ref=sums.at[pl.ds(pl.multiple_of(to * chunk, 8), chunk), :],
            dst_ref=parts.at[d],
            send_sem=send1.at[d],
            recv_sem=recv1.at[d],
            device_id=device(to),
            device_id_type=MESH,
        )

    mine = pl.ds(pl.multiple_of(rank * chunk, 8), chunk)

    def spread(d):
        to = lax.rem(rank + d, members)
        return pltpu.make_async_remote_copy(
            src_ref=piece,
            dst_ref=total.at[mine, :],
            send_sem=send2.at[d],
            recv_sem=recv2.at[d],
            device_id=device(to),
            device_id_type=MESH,
        )

    def start_pivots(d):
        return pltpu.make_async_remote_copy(
            src_ref=right_cat.at[pl.ds(0, pivot_rows), :],
            dst_ref=pivots.at[front],
            send_sem=send3.at[d],
            recv_sem=recv3.at[d],
            device_id=(leaf, lax.rem(front + d, front_count)),
            device_id_type=MESH,
        )

    def each(count, action):
        def body(d, _):
            action(d)
            return 0

        lax.fori_loop(1, count, body, 0)

    each(members, lambda d: scatter(d).start())
    if last:
        each(front_count, lambda d: start_pivots(d).start())
        pivots[front] = right_cat[:pivot_rows, :]
    piece[...] = sums[mine, :]

    def collect(d):
        scatter(d).wait_recv()
        piece[...] += parts[d]

    each(members, collect)
    each(members, lambda d: spread(d).start())
    total[mine, :] = piece[...]
    each(members, lambda d: spread(d).wait_recv())

    sketched = total[: 2 * width, :]
    cross = total[3 * width : 4 * width, :]
    upper = jnp.concatenate([total[2 * width : 3 * width, :], cross], axis=1)
    lower = jnp.concatenate([cross.T, total[4 * width : 5 * width, :]], axis=1)
    whole = jnp.concatenate([upper, lower], axis=0)
    applied = dot(whole, sketched, precision=HIGHEST_PREC)
    gram = dot(sketched, applied, ((0,), (0,)), precision=HIGHEST_PREC)
    inverted = inverse_factor(gram)
    scale = math.sqrt(members * rows)
    weights = dot(sketched, inverted, ((1,), (1,)), precision=HIGHEST_PREC)
    project = dot(applied, inverted, ((1,), (1,)), precision=HIGHEST_PREC)
    left_high, left_low = halves(weights * scale)
    right_high, right_low = halves(project / scale)

    if last:
        each(front_count, lambda d: start_pivots(d).wait_recv())
        first = pivots[0]
        right_piv = (dot(first, right_high) + dot(first, right_low)).astype(BF16)

    def out(step, _):
        here = pl.ds(pl.multiple_of(step * PIECE, PIECE), PIECE)
        left_rows = left_cat[here, :]
        right_rows = right_cat[here, :]
        left = (dot(left_rows, left_high) + dot(left_rows, left_low)).astype(BF16)
        left_out[here, :] = left
        right_out[here, :] = (dot(right_rows, right_high) + dot(right_rows, right_low)).astype(BF16)
        if last:
            updated = panel[here, :].astype(F32) - dot(left, right_piv, ((1,), (1,)))
            high, rest = halves(updated)
            panel_out[here, :] = (dot(high, inverse[...]) + dot(rest, inverse[...])).astype(BF16)
        return 0

    lax.fori_loop(0, rows // PIECE, out, 0)
    each(members, lambda d: scatter(d).wait_send())
    each(members, lambda d: spread(d).wait_send())
    if last:
        each(front_count, lambda d: start_pivots(d).wait_send())


def params(**more):
    return pltpu.CompilerParams(vmem_limit_bytes=VMEM_LIMIT, **more)


def on_device(child_u, child_v, sketch, map_own, map_peer, live_rows, front_panel, pivot_inverse):
    rows, width = child_u.shape
    level_count = sketch.shape[0]
    front_count = lax.axis_size("front")
    leaf_count = lax.axis_size("leaf")
    left, right = child_u, child_v
    narrow = jax.ShapeDtypeStruct((rows, width), BF16)
    cat = jax.ShapeDtypeStruct((rows, 2 * width), BF16)
    tables = [pltpu.VMEM((2 * rows, width), F32)] * 2
    for level in range(level_count):
        members = 2 ** (level + 1) * front_count
        chunk = -(-5 * width // (8 * members)) * 8
        live = live_rows[level].reshape(1, 1)
        left_sibling = from_partner(left, "leaf", level)
        right_sibling = from_partner(right, "leaf", level)
        with jax.named_scope("own_rows"):
            left_own, right_own = pl.pallas_call(
                own_kernel,
                out_shape=(narrow, narrow),
                in_specs=[SMEM_SPEC] * 2 + [VMEM_SPEC] * 2,
                out_specs=(VMEM_SPEC,) * 2,
                scratch_shapes=tables,
                compiler_params=params(),
                cost_estimate=pl.CostEstimate(
                    flops=10 * rows * width, bytes_accessed=20 * rows * width, transcendentals=0
                ),
            )(map_own[level], live, left, right)
        with jax.named_scope("peer_rows"):
            left_cat, right_cat, sums = pl.pallas_call(
                peer_kernel,
                out_shape=(cat, cat, jax.ShapeDtypeStruct((members * chunk, width), F32)),
                in_specs=[SMEM_SPEC] * 2 + [VMEM_SPEC] * 5,
                out_specs=(VMEM_SPEC,) * 3,
                scratch_shapes=tables,
                compiler_params=params(),
                cost_estimate=pl.CostEstimate(
                    flops=12 * rows * width * width, bytes_accessed=20 * rows * width,
                    transcendentals=0,
                ),
            )(
                map_peer[level], live, left_sibling, right_sibling, left_own, right_own,
                sketch[level],
            )
        last = level == level_count - 1
        operands = [sums, left_cat, right_cat]
        outs = [narrow, narrow]
        scratch = [
            pltpu.VMEM((members, chunk, width), F32),
            pltpu.VMEM((chunk, width), F32),
            pltpu.VMEM((members * chunk, width), F32),
        ]
        if last:
            operands += [front_panel, pivot_inverse]
            outs += [jax.ShapeDtypeStruct(front_panel.shape, BF16)]
            scratch += [pltpu.VMEM((front_count, pivot_inverse.shape[0], 2 * width), BF16)]
        scratch += [pltpu.SemaphoreType.DMA((members,))] * 4
        if last:
            scratch += [pltpu.SemaphoreType.DMA((front_count,))] * 2
        with jax.named_scope("group_sum_and_fronts"):
            results = pl.pallas_call(
                functools.partial(
                    front_kernel, level, pivot_inverse.shape[0] if last else 0,
                    leaf_count, front_count,
                ),
                out_shape=tuple(outs),
                in_specs=[VMEM_SPEC] * len(operands),
                out_specs=(VMEM_SPEC,) * len(outs),
                scratch_shapes=scratch,
                compiler_params=params(collective_id=level, has_side_effects=True),
                cost_estimate=pl.CostEstimate(
                    flops=16 * rows * width * width, bytes_accessed=20 * rows * width,
                    transcendentals=0,
                ),
            )(*operands)
        left, right = results[:2]
    return left, right, results[2]


def solution(mesh):
    placed = (
        P(("leaf", "front"), None),
        P(("leaf", "front"), None),
        P(None, ("leaf", "front"), None),
        P(None, ("leaf", "front")),
        P(None, ("leaf", "front")),
        P(None, ("leaf", "front")),
        P(("leaf", "front"), None),
        P("leaf", None),
    )
    return jax.shard_map(
        on_device,
        mesh=mesh,
        in_specs=placed,
        out_specs=(
            P(("leaf", "front"), None),
            P(("leaf", "front"), None),
            P(("leaf", "front"), None),
        ),
        check_vma=False,
    )
```

time: 875 us -> 339 us (0.39)
  waiting for transfers between devices: 474 us -> 158 us
  local copies, waits for them, and re-layouts: 198 us -> 14 us
  Pallas kernels: 0 us -> 160 us
  other arithmetic: 82 us -> 0 us
  matrix products: 66 us -> 0 us
  blocking collectives: 14.6 us -> 0 us
  between operations: 14.9 us -> 0.71 us
  starting transfers between devices: 17 us -> 5.48 us
    psum x9 -> x0, waiting for transfers between devices: 294 us -> none  [group_sum(): total = lax.psum(partial_sum, 'front')]
    gather x12 -> x0, local copies, waits for them, and re-layouts: 180 us -> none  [the longest x3 45.1 us: on_device(): sibling[1][map_other]]
    pallas_call x0 -> x9, Pallas kernels: none -> 160 us  [the longest x3 115 us: on_device(): pl.pallas_call(functools.partial(front_kernel, level, pivot_inverse.shape...]
    another operation x18 -> x0, other arithmetic: 73.5 us -> none  [the longest x9 37.2 us: on_device(): lower = jnp.linalg.cholesky(gram)]
    dot_general x17 -> x0, matrix products: 60 us -> none  [the longest x9 34.3 us: contract(): lax.dot_general(first, second, (((0,), (0,)), ((), ())), preferred_elemen...]
    ppermute x21 -> x6, waiting for transfers between devices: 179 us -> 158 us  [from_partner(): return lax.ppermute(block, axis, route)]
    psum x1 -> x0, blocking collectives: 14.6 us -> none  [broadcast(): return lax.psum(jnp.where(mine, shard, jnp.zeros_like(shard)), axis)]
    ppermute x21 -> x6, starting transfers between devices: 15.4 us -> 5.48 us  [from_partner(): return lax.ppermute(block, axis, route)]
  transfers between devices with their start and end apart: 30 -> 6, of which waited for: 27 -> 6; matrix products, arithmetic and copies ran while one was open for 17% -> 2% of each run, Pallas kernels for 0% -> 5%
where the time goes in v1:
time: 339 us; the launch traced here: 338 us
  Pallas kernels  160 us (47%)
  waiting for transfers between devices  158 us (47%)
  local copies, waits for them, and re-layouts  14 us (4%)
  starting transfers between devices  5.48 us (2%)
    ppermute x6, waiting for transfers between devices, from_partner(): return lax.ppermute(block, axis, route)  158 us
    pallas_call x3, Pallas kernels, on_device(): pl.pallas_call(functools.partial(front_kernel, level, pivot_inverse.shape...  115 us
    pallas_call x3, Pallas kernels, on_device(): pl.pallas_call(peer_kernel, out_shape=(cat, cat, jax.ShapeDtypeStruct((me...  29.4 us
    pallas_call x3, Pallas kernels, on_device(): pl.pallas_call(own_kernel, out_shape=(narrow, narrow), in_specs=[SMEM_SPE...  16.1 us
    unnamed x15, local copies, waits for them, and re-layouts  8.55 us
  transfers between devices with their start and end apart: 6, of which 6 were waited for; matrix products, arithmetic and copies ran while one was open for 2% of the time, Pallas kernels for 5%

profile of v1, /device:TPU:25, one launch (start us, length us, event | category | flops | bytes accessed | tf_op | source)
XLA Modules:
  0.0 338.4 jit_solution(14393251849439672574)
XLA Ops:
  0.6 1.3 collective-permute-start
  1.9 0.2 collective-permute-start.1
  2.2 1.0 fusion
  3.2 1.0 fusion.1
  4.2 1.4 fusion.2
  5.5 0.0 copy-start.2
  5.5 1.2 copy-done.2
  6.7 0.0 copy-start.3
  6.8 1.2 copy-done.3
  8.0 5.2 %own_rows.3 = (bf16[4096,128]{1,0:T(8,128)(2,1)S(1)}, bf16[4096,128]{1,0:T(8,128)(2,1)S(1)}) custom-call(s32[4096]{0:T(1024)S(1)} %bitcast.20, s32[1,1]{1,0:T(1,128)} %bitcast.11.live_ref, bf16[4096,128]{1,0:T(8,128)(2,1)S(1)} %copy-done.2, bf16[4096,128]{1,0:T(8,128)(2,1)S(1)} %copy-done.3), custom_call_target="tpu_custom_call" | custom-call | flops 5242880 | bytes 10485760 | tf_op jit(solution)/shard_map/own_rows/pallas_call | solution.py:298
  13.2 2.1 slice_bitcast_fusion
  15.3 9.7 %collective-permute-done.left_ref = bf16[4096,128]{1,0:T(8,128)(2,1)S(1)} collective-permute-done((bf16[4096,128]{1,0:T(8,128)(2,1)}, bf16[4096,128]{1,0:T(8,128)(2,1)S(1)}, u32[]{:S(2)}, u32[]{:S(2)}) %collective-permute-start) | collective-permute-done | bytes 1048608 | tf_op jit(solution)/shard_map/ppermute | solution.py:30
  24.9 22.5 %collective-permute-done.1.right_ref = bf16[4096,128]{1,0:T(8,128)(2,1)S(1)} collective-permute-done((bf16[4096,128]{1,0:T(8,128)(2,1)}, bf16[4096,128]{1,0:T(8,128)(2,1)S(1)}, u32[]{:S(2)}, u32[]{:S(2)}) %collective-permute-start.1) | collective-permute-done | bytes 1048608 | tf_op jit(solution)/shard_map/ppermute | solution.py:30
  47.4 9.5 %peer_rows.3 = (bf16[4096,256]{1,0:T(8,128)(2,1)}, bf16[4096,256]{1,0:T(8,128)(2,1)}, f32[640,128]{1,0:T(8,128)S(1)}) custom-call(s32[4096]{0:T(1024)S(1)} %bitcast.19, s32[1,1]{1,0:T(1,128)} %bitcast.11.live_ref, bf16[4096,128]{1,0:T(8,128)(2,1)S(1)} %collective-permute-done.left_ref, bf16[4096,128]{1,0:T(8,128)(2,1)S(1)} %collective-permute-done.1.right_ref, ...), custom_call_target="tpu_custom_call" | custom-call | flops 805306368 | bytes 10485760 | tf_op jit(solution)/shard_map/peer_rows/pallas_call | solution.py:310
  57.0 0.0 copy-start
  57.0 1.6 copy-done
  58.5 33.0 %group_sum_and_fronts.3 = (bf16[4096,128]{1,0:T(8,128)(2,1)S(1)}, bf16[4096,128]{1,0:T(8,128)(2,1)S(1)}) custom-call(f32[640,128]{1,0:T(8,128)S(1)} %get-tuple-element.24.sums, bf16[4096,256]{1,0:T(8,128)(2,1)S(1)} %copy-done, bf16[4096,256]{1,0:T(8,128)(2,1)} %get-tuple-element.26.right_cat), custom_call_target="tpu_custom_call" | custom-call | flops 1073741824 | bytes 10485760 | tf_op jit(solution)/shard_map/group_sum_and_fronts/pallas_call | solution.py:341
  91.6 1.2 collective-permute-start.2
  92.8 0.3 collective-permute-start.3
  93.1 6.4 %own_rows.4 = (bf16[4096,128]{1,0:T(8,128)(2,1)S(1)}, bf16[4096,128]{1,0:T(8,128)(2,1)S(1)}) custom-call(s32[4096]{0:T(1024)S(1)} %bitcast.18, s32[1,1]{1,0:T(1,128)} %bitcast.10.live_ref, bf16[4096,128]{1,0:T(8,128)(2,1)S(1)} %get-tuple-element.27.left_ref, bf16[4096,128]{1,0:T(8,128)(2,1)S(1)} %get-tuple-element.28.right_ref), custom_call_target="tpu_custom_call" | custom-call | flops 5242880 | bytes 10485760 | tf_op jit(solution)/shard_map/own_rows/pallas_call | solution.py:298
  99.5 16.7 %collective-permute-done.2.left_ref = bf16[4096,128]{1,0:T(8,128)(2,1)S(1)} collective-permute-done((bf16[4096,128]{1,0:T(8,128)(2,1)S(1)}, bf16[4096,128]{1,0:T(8,128)(2,1)S(1)}, u32[]{:S(2)}, u32[]{:S(2)}) %collective-permute-start.2) | collective-permute-done | bytes 1048608 | tf_op jit(solution)/shard_map/ppermute | solution.py:30
  116.2 22.5 %collective-permute-done.3.right_ref = bf16[4096,128]{1,0:T(8,128)(2,1)S(1)} collective-permute-done((bf16[4096,128]{1,0:T(8,128)(2,1)S(1)}, bf16[4096,128]{1,0:T(8,128)(2,1)S(1)}, u32[]{:S(2)}, u32[]{:S(2)}) %collective-permute-start.3) | collective-permute-done | bytes 1048608 | tf_op jit(solution)/shard_map/ppermute | solution.py:30
  138.7 10.9 %peer_rows.4 = (bf16[4096,256]{1,0:T(8,128)(2,1)}, bf16[4096,256]{1,0:T(8,128)(2,1)}, f32[640,128]{1,0:T(8,128)S(1)}) custom-call(s32[4096]{0:T(1024)S(1)} %bitcast.17, s32[1,1]{1,0:T(1,128)} %bitcast.10.live_ref, bf16[4096,128]{1,0:T(8,128)(2,1)S(1)} %collective-permute-done.2.left_ref, bf16[4096,128]{1,0:T(8,128)(2,1)S(1)} %collective-permute-done.3.right_ref, ...), custom_call_target="tpu_custom_call" | custom-call | flops 805306368 | bytes 10485760 | tf_op jit(solution)/shard_map/peer_rows/pallas_call | solution.py:310
  149.6 0.0 copy-start.1
  149.6 1.6 copy-done.1
  151.2 33.3 %group_sum_and_fronts.4 = (bf16[4096,128]{1,0:T(8,128)(2,1)S(1)}, bf16[4096,128]{1,0:T(8,128)(2,1)S(1)}) custom-call(f32[640,128]{1,0:T(8,128)S(1)} %get-tuple-element.31.sums, bf16[4096,256]{1,0:T(8,128)(2,1)S(1)} %copy-done.1, bf16[4096,256]{1,0:T(8,128)(2,1)} %get-tuple-element.33.right_cat), custom_call_target="tpu_custom_call" | custom-call | flops 1073741824 | bytes 10485760 | tf_op jit(solution)/shard_map/group_sum_and_fronts/pallas_call | solution.py:341
  184.5 0.1 collective-permute-start.4
  184.6 2.4 collective-permute-start.5
  186.9 4.5 %own_rows.5 = (bf16[4096,128]{1,0:T(8,128)(2,1)S(1)}, bf16[4096,128]{1,0:T(8,128)(2,1)S(1)}) custom-call(s32[4096]{0:T(1024)S(1)} %bitcast.16, s32[1,1]{1,0:T(1,128)} %bitcast.9.live_ref, bf16[4096,128]{1,0:T(8,128)(2,1)S(1)} %get-tuple-element.34.left_ref, bf16[4096,128]{1,0:T(8,128)(2,1)S(1)} %get-tuple-element.35.right_ref), custom_call_target="tpu_custom_call" | custom-call | flops 5242880 | bytes 10485760 | tf_op jit(solution)/shard_map/own_rows/pallas_call | solution.py:298
  191.4 64.0 %collective-permute-done.4.left_ref = bf16[4096,128]{1,0:T(8,128)(2,1)S(1)} collective-permute-done((bf16[4096,128]{1,0:T(8,128)(2,1)S(1)}, bf16[4096,128]{1,0:T(8,128)(2,1)S(1)}, u32[]{:S(2)}, u32[]{:S(2)}) %collective-permute-start.4) | collective-permute-done | bytes 1048608 | tf_op jit(solution)/shard_map/ppermute | solution.py:30
  255.4 22.5 %collective-permute-done.5.right_ref = bf16[4096,128]{1,0:T(8,128)(2,1)S(1)} collective-permute-done((bf16[4096,128]{1,0:T(8,128)(2,1)S(1)}, bf16[4096,128]{1,0:T(8,128)(2,1)S(1)}, u32[]{:S(2)}, u32[]{:S(2)}) %collective-permute-start.5) | collective-permute-done | bytes 1048608 | tf_op jit(solution)/shard_map/ppermute | solution.py:30
  277.9 0.0 copy-start.4
  277.9 0.0 copy-start.5
  277.9 8.9 %peer_rows.5 = (bf16[4096,256]{1,0:T(8,128)(2,1)}, bf16[4096,256]{1,0:T(8,128)(2,1)}, f32[768,128]{1,0:T(8,128)S(1)}) custom-call(s32[4096]{0:T(1024)S(1)} %bitcast.15, s32[1,1]{1,0:T(1,128)} %bitcast.9.live_ref, bf16[4096,128]{1,0:T(8,128)(2,1)S(1)} %collective-permute-done.4.left_ref, bf16[4096,128]{1,0:T(8,128)(2,1)S(1)} %collective-permute-done.5.right_ref, ...), custom_call_target="tpu_custom_call" | custom-call | flops 805306368 | bytes 10485760 | tf_op jit(solution)/shard_map/peer_rows/pallas_call | solution.py:310
  286.8 0.0 copy-done.4
  286.8 0.0 copy-done.5
  286.8 48.7 %group_sum_and_fronts.5 = (bf16[4096,128]{1,0:T(8,128)(2,1)S(1)}, bf16[4096,128]{1,0:T(8,128)(2,1)S(1)}, bf16[4096,128]{1,0:T(8,128)(2,1)S(1)}) custom-call(f32[768,128]{1,0:T(8,128)S(1)} %get-tuple-element.38.sums, bf16[4096,256]{1,0:T(8,128)(2,1)} %get-tuple-element.39.left_cat, bf16[4096,256]{1,0:T(8,128)(2,1)} %get-tuple-element.40.right_cat, ...), custom_call_target="tpu_custom_call" | custom-call | flops 1073741824 | bytes 10485760 | tf_op jit(solution)/shard_map/group_sum_and_fronts/pallas_call | solution.py:341
  335.5 1.0 copy.20
  336.5 1.0 copy.21
  337.4 1.0 copy.22
Async XLA Ops:
  0.6 24.3 %collective-permute-start = (bf16[4096,128]{1,0:T(8,128)(2,1)}, bf16[4096,128]{1,0:T(8,128)(2,1)S(1)}, u32[]{:S(2)}, u32[]{:S(2)}) collective-permute-start(bf16[4096,128]{1,0:T(8,128)(2,1)} %left_ref.1), channel_id=1, source_target_pairs={{0,4},{4,0},{8,12},{12,8},{16,20},{20,16},{24,28},{28,24},{1,5},{5... | collective-permute-start | bytes 3145736 | tf_op jit(solution)/shard_map/ppermute | solution.py:30
  1.9 45.5 %collective-permute-start.1 = (bf16[4096,128]{1,0:T(8,128)(2,1)}, bf16[4096,128]{1,0:T(8,128)(2,1)S(1)}, u32[]{:S(2)}, u32[]{:S(2)}) collective-permute-start(bf16[4096,128]{1,0:T(8,128)(2,1)} %right_ref.1), channel_id=1, source_target_pairs={{0,4},{4,0},{8,12},{12,8},{16,20},{20,16},{24,28},{28,24},{1,5},{5... | collective-permute-start | bytes 3145736 | tf_op jit(solution)/shard_map/ppermute | solution.py:30
  5.5 1.2 copy-start.2
  6.7 1.2 copy-start.3
  57.0 1.6 copy-start
  91.6 24.7 %collective-permute-start.2 = (bf16[4096,128]{1,0:T(8,128)(2,1)S(1)}, bf16[4096,128]{1,0:T(8,128)(2,1)S(1)}, u32[]{:S(2)}, u32[]{:S(2)}) collective-permute-start(bf16[4096,128]{1,0:T(8,128)(2,1)S(1)} %get-tuple-element.27.left_ref), channel_id=1, source_target_pairs={{0,8},{8,0},{4,12},{12,4},{16,24},{24,16},{20,28},{28,20},{1,9},{9... | collective-permute-start | bytes 3145736 | tf_op jit(solution)/shard_map/ppermute | solution.py:30
  92.8 45.9 %collective-permute-start.3 = (bf16[4096,128]{1,0:T(8,128)(2,1)S(1)}, bf16[4096,128]{1,0:T(8,128)(2,1)S(1)}, u32[]{:S(2)}, u32[]{:S(2)}) collective-permute-start(bf16[4096,128]{1,0:T(8,128)(2,1)S(1)} %get-tuple-element.28.right_ref), channel_id=1, source_target_pairs={{0,8},{8,0},{4,12},{12,4},{16,24},{24,16},{20,28},{28,20},{1,9},{9... | collective-permute-start | bytes 3145736 | tf_op jit(solution)/shard_map/ppermute | solution.py:30
  149.6 1.6 copy-start.1
  184.5 70.9 %collective-permute-start.4 = (bf16[4096,128]{1,0:T(8,128)(2,1)S(1)}, bf16[4096,128]{1,0:T(8,128)(2,1)S(1)}, u32[]{:S(2)}, u32[]{:S(2)}) collective-permute-start(bf16[4096,128]{1,0:T(8,128)(2,1)S(1)} %get-tuple-element.34.left_ref), channel_id=1, source_target_pairs={{0,16},{16,0},{4,20},{20,4},{8,24},{24,8},{12,28},{28,12},{1,17},{... | collective-permute-start | bytes 3145736 | tf_op jit(solution)/shard_map/ppermute | solution.py:30
  184.6 93.3 %collective-permute-start.5 = (bf16[4096,128]{1,0:T(8,128)(2,1)S(1)}, bf16[4096,128]{1,0:T(8,128)(2,1)S(1)}, u32[]{:S(2)}, u32[]{:S(2)}) collective-permute-start(bf16[4096,128]{1,0:T(8,128)(2,1)S(1)} %get-tuple-element.35.right_ref), channel_id=1, source_target_pairs={{0,16},{16,0},{4,20},{20,4},{8,24},{24,8},{12,28},{28,12},{1,17},{... | collective-permute-start | bytes 3145736 | tf_op jit(solution)/shard_map/ppermute | solution.py:30
  277.9 8.9 %copy-start.4 = (bf16[4096,128]{1,0:T(8,128)(2,1)S(1)}, bf16[4096,128]{1,0:T(8,128)(2,1)}, u32[]{:S(2)}) copy-start(bf16[4096,128]{1,0:T(8,128)(2,1)} %refs_0_.1) | copy-start | bytes 3145732
  277.9 8.9 %copy-start.5 = (bf16[128,128]{1,0:T(8,128)(2,1)S(1)}, bf16[128,128]{1,0:T(8,128)(2,1)}, u32[]{:S(2)}) copy-start(bf16[128,128]{1,0:T(8,128)(2,1)} %refs_1_.1) | copy-start | bytes 98308

commit v2 on v1

v2 whole, which is shorter than its diff:
```python
import functools
import math

import jax
import jax.numpy as jnp
from jax import lax
from jax.experimental import pallas as pl
from jax.experimental.pallas import tpu as pltpu
from jax.sharding import PartitionSpec as P

BF16 = jnp.bfloat16
F32 = jnp.float32
HIGHEST_PREC = lax.Precision.HIGHEST
MESH = pl.DeviceIdType.MESH
VMEM_LIMIT = 48 * 1024 * 1024
UNROLL = 32
PIECE = 512

VMEM_SPEC = pl.BlockSpec(memory_space=pltpu.VMEM)
SMEM_SPEC = pl.BlockSpec(memory_space=pltpu.SMEM)


def from_partner(block, axis, stride):
    count = lax.axis_size(axis)
    route = []
    for low in range(count):
        high = low | 1 << stride
        if high != low and high < count:
            route += [(low, high), (high, low)]
    return lax.ppermute(block, axis, route)


def dot(first, second, dims=((1,), (0,)), precision=None):
    return lax.dot_general(
        first, second, (dims, ((), ())), preferred_element_type=F32, precision=precision
    )


def halves(wide):
    high = wide.astype(BF16)
    return high, (wide - high.astype(F32)).astype(BF16)


def fill_pairs(left_ref, right_ref, table):
    def fill(step, _):
        at = pl.multiple_of(step * PIECE, PIECE)
        table[pl.ds(2 * at, PIECE, stride=2), :] = left_ref[pl.ds(at, PIECE), :].astype(F32)
        table[pl.ds(2 * at + 1, PIECE, stride=2), :] = right_ref[pl.ds(at, PIECE), :].astype(F32)
        return 0

    lax.fori_loop(0, left_ref.shape[0] // PIECE, fill, 0)


def fill_single(source_ref, table):
    def fill(step, _):
        here = pl.ds(pl.multiple_of(step * PIECE, PIECE), PIECE)
        table[here, :] = source_ref[here, :].astype(F32)
        return 0

    lax.fori_loop(0, source_ref.shape[0] // PIECE, fill, 0)


def pick_rows(index_ref, live, table, picked, wide):
    def pick(step, _):
        base = step * UNROLL
        loaded = []
        for j in range(UNROLL):
            loaded.append(table[pl.ds(wide * index_ref[base + j], wide), :])
        for j in range(UNROLL):
            picked[pl.ds(wide * (base + j), wide), :] = loaded[j]
        return 0

    lax.fori_loop(0, (live + UNROLL - 1) // UNROLL, pick, 0)


def keep_rows(at, live, width):
    return lax.broadcasted_iota(jnp.int32, (PIECE, width), 0) + at < live


def pieces(rows, action):
    def body(step, _):
        action(pl.multiple_of(step * PIECE, PIECE))
        return 0

    lax.fori_loop(0, rows // PIECE, body, 0)


def own_kernel(index_ref, live_ref, left_ref, right_ref, left_own, right_own, table, picked):
    rows, width = left_ref.shape
    live = live_ref[0, 0]
    fill_pairs(left_ref, right_ref, table)
    pick_rows(index_ref, live, table, picked, 2)

    def store(at):
        keep = keep_rows(at, live, width)
        here = pl.ds(at, PIECE)
        first = picked[pl.ds(2 * at, PIECE, stride=2), :]
        second = picked[pl.ds(2 * at + 1, PIECE, stride=2), :]
        left_own[here, :] = jnp.where(keep, first, 0.0).astype(BF16)
        right_own[here, :] = jnp.where(keep, second, 0.0).astype(BF16)

    pieces(rows, store)


def sketch_kernel(
    other_ref, right_ref, right_own, sketch_ref, other_sketch, sums, table, picked
):
    rows, width = right_ref.shape
    live = other_ref[rows]
    fill_single(right_ref, table)
    pick_rows(other_ref, live, table, picked, 1)
    sums[...] = jnp.zeros_like(sums)

    def add(at):
        here = pl.ds(at, PIECE)
        sums[:width, :] += dot(right_own[here, :], sketch_ref[here, :], ((0,), (0,)))
        given = jnp.where(keep_rows(at, live, width), picked[here, :], 0.0).astype(BF16)
        sums[width:, :] += dot(given, other_sketch[here, :], ((0,), (0,)))

    pieces(rows, add)


def left_kernel(index_ref, live_ref, left_ref, left_own, left_cat, sums, table, picked):
    rows, width = left_ref.shape
    live = live_ref[0, 0]
    fill_single(left_ref, table)
    pick_rows(index_ref, live, table, picked, 1)
    sums[...] = jnp.zeros_like(sums)

    def add(at):
        here = pl.ds(at, PIECE)
        given = jnp.where(keep_rows(at, live, width), picked[here, :], 0.0).astype(BF16)
        left_cat[here, :width] = left_own[here, :]
        left_cat[here, width:] = given
        both = left_cat[here, :]
        gram = dot(both, both, ((0,), (0,)))
        sums[:width, :] += gram[:width, :width]
        sums[width : 2 * width, :] += gram[:width, width:]
        sums[2 * width :, :] += gram[width:, width:]

    pieces(rows, add)


def right_kernel(
    index_ref, live_ref, right_ref, right_own, project_high, project_low, right_out, table, picked
):
    rows, width = right_ref.shape
    live = live_ref[0, 0]
    fill_single(right_ref, table)
    pick_rows(index_ref, live, table, picked, 1)

    def out(at):
        here = pl.ds(at, PIECE)
        given = jnp.where(keep_rows(at, live, width), picked[here, :], 0.0).astype(BF16)
        both = jnp.concatenate([right_own[here, :], given], axis=1)
        right_out[here, :] = (dot(both, project_high[...]) + dot(both, project_low[...])).astype(BF16)

    pieces(rows, out)


def inverse_factor(gram):
    size = gram.shape[0]
    tiles = [gram[8 * t : 8 * t + 8, :] for t in range(size // 8)]
    lane = lax.broadcasted_iota(jnp.int32, (8, size), 1)
    sublane = lax.broadcasted_iota(jnp.int32, (8, size), 0)
    pivots = [jnp.ones((8, size), F32) for _ in tiles]
    for k in range(size):
        own, within = divmod(k, 8)
        row = tiles[own][within : within + 1, :]
        pivot = row[:, k : k + 1]
        pivots[own] = jnp.where(sublane == within, pivot, pivots[own])
        inverse = 1.0 / pivot
        scaled = jnp.where(lane[:1] == k, inverse, row * inverse)
        for t in range(own, size // 8):
            column = tiles[t][:, k : k + 1]
            old = jnp.where(lane == k, 0.0, tiles[t])
            new = old - column * scaled
            if t == own:
                new = jnp.where(sublane > within, new, tiles[t])
                new = jnp.where((sublane == within) & (lane == k), 1.0, new)
            tiles[t] = new
    wide = [
        jnp.where(lane <= sublane + 8 * t, tile, 0.0) * lax.rsqrt(pivots[t])
        for t, tile in enumerate(tiles)
    ]
    return jnp.concatenate(wide, axis=0)


def greet(peers):
    barrier = pltpu.get_barrier_semaphore()
    count = peers[0]

    def signal(d, _):
        pl.semaphore_signal(barrier, inc=1, device_id=peers[1](d), device_id_type=MESH)
        return 0

    lax.fori_loop(1, count, signal, 0)
    pl.semaphore_wait(barrier, count - 1)


def each(count, action):
    def body(d, _):
        action(d)
        return 0

    lax.fori_loop(1, count, body, 0)


def factor_kernel(
    level, front_count, sketch_sums, gram_sums, left_cat, left_out, project_high, project_low,
    local, parts, piece, total, send1, recv1, send2, recv2,
):
    rows = left_cat.shape[0]
    width = left_cat.shape[1] // 2
    subtrees = 2 ** (level + 1)
    members = subtrees * front_count
    chunk = piece.shape[0]
    leaf, front = lax.axis_index("leaf"), lax.axis_index("front")
    low = lax.rem(leaf, subtrees)
    rank = low * front_count + front

    def device(d):
        place = lax.rem(rank + d, members)
        return (leaf - low + place // front_count, lax.rem(place, front_count))

    local[: 2 * width, :] = sketch_sums[...]
    local[2 * width : 5 * width, :] = gram_sums[...]
    if local.shape[0] > 5 * width:
        local[5 * width :, :] = jnp.zeros((local.shape[0] - 5 * width, width), F32)
    greet((members, device))

    def scatter(d):
        to = lax.rem(rank + d, members)
        return pltpu.make_async_remote_copy(
            src_ref=local.at[pl.ds(pl.multiple_of(to * chunk, 8), chunk), :],
            dst_ref=parts.at[d],
            send_sem=send1.at[d],
            recv_sem=recv1.at[d],
            device_id=device(d),
            device_id_type=MESH,
        )

    mine = pl.ds(pl.multiple_of(rank * chunk, 8), chunk)

    def spread(d):
        return pltpu.make_async_remote_copy(
            src_ref=piece,
            dst_ref=total.at[mine, :],
            send_sem=send2.at[d],
            recv_sem=recv2.at[d],
            device_id=device(d),
            device_id_type=MESH,
        )

    each(members, lambda d: scatter(d).start())
    piece[...] = local[mine, :]

    def collect(d):
        scatter(d).wait_recv()
        piece[...] += parts[d]

    each(members, collect)
    each(members, lambda d: spread(d).start())
    total[mine, :] = piece[...]
    each(members, lambda d: spread(d).wait_recv())

    sketched = total[: 2 * width, :]
    cross = total[3 * width : 4 * width, :]
    upper = jnp.concatenate([total[2 * width : 3 * width, :], cross], axis=1)
    lower = jnp.concatenate([cross.T, total[4 * width : 5 * width, :]], axis=1)
    whole = jnp.concatenate([upper, lower], axis=0)
    applied = dot(whole, sketched, precision=HIGHEST_PREC)
    gram = dot(sketched, applied, ((0,), (0,)), precision=HIGHEST_PREC)
    inverted = inverse_factor(gram)
    scale = math.sqrt(members * rows)
    weights = dot(sketched, inverted, ((1,), (1,)), precision=HIGHEST_PREC)
    left_high, left_low = halves(weights * scale)

    def out(at):
        here = pl.ds(at, PIECE)
        left_rows = left_cat[here, :]
        left_out[here, :] = (dot(left_rows, left_high) + dot(left_rows, left_low)).astype(BF16)

    pieces(rows, out)
    project = dot(applied, inverted, ((1,), (1,)), precision=HIGHEST_PREC)
    high, rest = halves(project / scale)
    project_high[...] = high
    project_low[...] = rest
    each(members, lambda d: scatter(d).wait_send())
    each(members, lambda d: spread(d).wait_send())


def panel_kernel(front_count, left, right, panel, inverse, panel_out, pivots, send, recv):
    leaf, front = lax.axis_index("leaf"), lax.axis_index("front")
    pivot_rows = inverse.shape[0]

    def device(d):
        return (leaf, lax.rem(front + d, front_count))

    greet((front_count, device))

    def share(d):
        return pltpu.make_async_remote_copy(
            src_ref=right.at[pl.ds(0, pivot_rows), :],
            dst_ref=pivots.at[front],
            send_sem=send.at[d],
            recv_sem=recv.at[d],
            device_id=device(d),
            device_id_type=MESH,
        )

    each(front_count, lambda d: share(d).start())
    pivots[front] = right[:pivot_rows, :]
    each(front_count, lambda d: share(d).wait_recv())
    right_piv = pivots[0]

    def out(at):
        here = pl.ds(at, PIECE)
        updated = panel[here, :].astype(F32) - dot(left[here, :], right_piv, ((1,), (1,)))
        high, rest = halves(updated)
        panel_out[here, :] = (dot(high, inverse[...]) + dot(rest, inverse[...])).astype(BF16)

    pieces(left.shape[0], out)
    each(front_count, lambda d: share(d).wait_send())


def call(kernel, outs, operands, scalars, scratch, flops, moved, **more):
    return pl.pallas_call(
        kernel,
        out_shape=outs,
        in_specs=[SMEM_SPEC] * scalars + [VMEM_SPEC] * (len(operands) - scalars),
        out_specs=tuple(VMEM_SPEC for _ in outs),
        scratch_shapes=scratch,
        compiler_params=pltpu.CompilerParams(vmem_limit_bytes=VMEM_LIMIT, **more),
        cost_estimate=pl.CostEstimate(flops=flops, bytes_accessed=moved, transcendentals=0),
    )(*operands)


def on_device(child_u, child_v, sketch, map_own, map_peer, live_rows, front_panel, pivot_inverse):
    rows, width = child_u.shape
    level_count = sketch.shape[0]
    front_count = lax.axis_size("front")
    left, right = child_u, child_v
    narrow = jax.ShapeDtypeStruct((rows, width), BF16)
    cat = jax.ShapeDtypeStruct((rows, 2 * width), BF16)
    small = jax.ShapeDtypeStruct((2 * width, width), BF16)
    pairs = [pltpu.VMEM((2 * rows, width), F32)] * 2
    singles = [pltpu.VMEM((rows, width), F32)] * 2
    unit = 22_000_000
    others = []
    for level in range(level_count):
        tail = jnp.broadcast_to(live_rows[level], (width,))
        others.append(from_partner(jnp.concatenate([map_peer[level], tail]), "leaf", level))
    left_sibling = from_partner(left, "leaf", 0)
    other_sketch = [from_partner(sketch[level], "leaf", level) for level in range(level_count)]
    for level in range(level_count):
        members = 2 ** (level + 1) * front_count
        chunk = -(-5 * width // (8 * members)) * 8
        live = live_rows[level].reshape(1, 1)
        if level:
            left_sibling = from_partner(left, "leaf", level)
        right_sibling = from_partner(right, "leaf", level)
        with jax.named_scope("own_rows"):
            left_own, right_own = call(
                own_kernel, (narrow, narrow), [map_own[level], live, left, right], 2, pairs,
                rows * width, unit,
            )
        with jax.named_scope("sketch_sums"):
            (sketch_sums,) = call(
                sketch_kernel, (jax.ShapeDtypeStruct((2 * width, width), F32),),
                [others[level], right, right_own, sketch[level], other_sketch[level]],
                1, singles, 4 * rows * width * width, unit,
            )
        with jax.named_scope("left_rows"):
            left_cat, gram_sums = call(
                left_kernel, (cat, jax.ShapeDtypeStruct((3 * width, width), F32)),
                [map_peer[level], live, left_sibling, left_own], 2, singles,
                8 * rows * width * width, unit,
            )
        if level == 0:
            (gram_sums, sketch_sums), others[2:], other_sketch[2:] = lax.optimization_barrier(
                ((gram_sums, sketch_sums), others[2:], other_sketch[2:])
            )
        with jax.named_scope("group_sum_and_factor"):
            left, project_high, project_low = call(
                functools.partial(factor_kernel, level, front_count),
                (narrow, small, small), [sketch_sums, gram_sums, left_cat], 0,
                [
                    pltpu.VMEM((members * chunk, width), F32),
                    pltpu.VMEM((members, chunk, width), F32),
                    pltpu.VMEM((chunk, width), F32),
                    pltpu.VMEM((members * chunk, width), F32),
                ]
                + [pltpu.SemaphoreType.DMA((members,))] * 4,
                8 * rows * width * width, 4 * unit,
                collective_id=level, has_side_effects=True,
            )
        if level == 0:
            (left, project_high), others[1:], other_sketch[1:] = lax.optimization_barrier(
                ((left, project_high), others[1:], other_sketch[1:])
            )
        with jax.named_scope("right_rows"):
            (right,) = call(
                right_kernel, (narrow,),
                [map_peer[level], live, right_sibling, right_own, project_high, project_low],
                2, singles, 8 * rows * width * width, unit,
            )
    with jax.named_scope("panel"):
        (panel_out,) = call(
            functools.partial(panel_kernel, front_count),
            (jax.ShapeDtypeStruct(front_panel.shape, BF16),),
            [left, right, front_panel, pivot_inverse], 0,
            [pltpu.VMEM((front_count,) + pivot_inverse.shape, BF16)]
            + [pltpu.SemaphoreType.DMA((front_count,))] * 2,
            8 * rows * width * width, unit,
            collective_id=level_count, has_side_effects=True,
        )
    return left, right, panel_out


def solution(mesh):
    placed = (
        P(("leaf", "front"), None),
        P(("leaf", "front"), None),
        P(None, ("leaf", "front"), None),
        P(None, ("leaf", "front")),
        P(None, ("leaf", "front")),
        P(None, ("leaf", "front")),
        P(("leaf", "front"), None),
        P("leaf", None),
    )
    return jax.shard_map(
        on_device,
        mesh=mesh,
        in_specs=placed,
        out_specs=(
            P(("leaf", "front"), None),
            P(("leaf", "front"), None),
            P(("leaf", "front"), None),
        ),
        check_vma=False,
    )
```

time: 339 us -> 331 us (0.976)
  waiting for transfers between devices: 158 us -> 99.9 us
  Pallas kernels: 160 us -> 212 us
  local copies, waits for them, and re-layouts: 14 us -> 7.87 us
    ppermute x6 -> x12, waiting for transfers between devices: 158 us -> 99.9 us  [from_partner(): return lax.ppermute(block, axis, route)]
    pallas_call x9 -> x16, Pallas kernels: 160 us -> 212 us  [call(): pl.pallas_call(kernel, out_shape=outs, in_specs=[SMEM_SPEC] * scalars + [...]
    unnamed x15 -> x18, local copies, waits for them, and re-layouts: 8.55 us -> 3.2 us
    ppermute x6 -> x12, starting transfers between devices: 5.48 us -> 8.8 us  [from_partner(): return lax.ppermute(block, axis, route)]
  transfers between devices with their start and end apart: 6 -> 12, of which waited for: 6 -> 4; matrix products, arithmetic and copies ran while one was open for 2% -> 1% of each run, Pallas kernels for 5% -> 60%
where the time goes in v2:
time: 331 us; the launch traced here: 330 us
  Pallas kernels  212 us (64%)
  waiting for transfers between devices  99.9 us (30%)
  starting transfers between devices  8.8 us (3%)
  local copies, waits for them, and re-layouts  7.87 us (2%)
    pallas_call x16, Pallas kernels, call(): pl.pallas_call(kernel, out_shape=outs, in_specs=[SMEM_SPEC] * scalars + [...  212 us
    ppermute x12, waiting for transfers between devices, from_partner(): return lax.ppermute(block, axis, route)  99.9 us
    ppermute x12, starting transfers between devices, from_partner(): return lax.ppermute(block, axis, route)  8.8 us
  transfers between devices with their start and end apart: 12, of which 4 were waited for; matrix products, arithmetic and copies ran while one was open for 1% of the time, Pallas kernels for 60%

profile of v2, /device:TPU:25, one launch (start us, length us, event | category | flops | bytes accessed | tf_op | source)
XLA Modules:
  0.0 329.8 jit_solution(11631499949418379657)
XLA Ops:
  0.7 1.3 collective-permute-start
  2.0 2.1 slice_bitcast_fusion
  4.0 0.4 collective-permute-start.2
  4.5 0.1 collective-permute-start.4
  4.5 0.1 collective-permute-start.6
  4.6 1.2 collective-permute-start.7
  5.9 0.6 fusion.2
  6.5 0.6 concatenate.9
  7.1 0.7 concatenate.10
  7.8 0.7 concatenate.11
  8.5 7.0 %own_rows.3 = (bf16[4096,128]{1,0:T(8,128)(2,1)S(1)}, bf16[4096,128]{1,0:T(8,128)(2,1)S(1)}) custom-call(s32[4096]{0:T(1024)S(1)} %bitcast.32, s32[1,1]{1,0:T(1,128)} %bitcast.12.live_ref, bf16[4096,128]{1,0:T(8,128)(2,1)S(1)} %copy-done.2, bf16[4096,128]{1,0:T(8,128)(2,1)S(1)} %copy-done), custom_call_target="tpu_custom_call" | custom-call | flops 524288 | bytes 22000000 | tf_op jit(solution)/shard_map/own_rows/pallas_call | solution.py:328
  15.5 9.5 %collective-permute-done.left_ref = bf16[4096,128]{1,0:T(8,128)(2,1)S(1)} collective-permute-done((bf16[4096,128]{1,0:T(8,128)(2,1)}, bf16[4096,128]{1,0:T(8,128)(2,1)S(1)}, u32[]{:S(2)}, u32[]{:S(2)}) %collective-permute-start) | collective-permute-done | bytes 1048608 | tf_op jit(solution)/shard_map/ppermute | solution.py:30
  25.0 1.2 collective-permute-start.1
  26.2 7.9 %left_rows.3 = (bf16[4096,256]{1,0:T(8,128)(2,1)S(1)}, f32[384,128]{1,0:T(8,128)S(1)}) custom-call(s32[4096]{0:T(1024)S(1)} %bitcast.28, s32[1,1]{1,0:T(1,128)} %bitcast.12.live_ref, bf16[4096,128]{1,0:T(8,128)(2,1)S(1)} %collective-permute-done.left_ref, bf16[4096,128]{1,0:T(8,128)(2,1)S(1)} %get-tuple-element.34.left_own), custom_call_target="tpu_custom_call" | custom-call | flops 536870912 | bytes 22000000 | tf_op jit(solution)/shard_map/left_rows/pallas_call | solution.py:328
  34.1 36.4 %collective-permute-done.1.other_ref = s32[4224]{0:T(1024)S(1)} collective-permute-done((s32[4224]{0:T(1024)S(1)}, s32[4224]{0:T(1024)S(1)}, u32[]{:S(2)}, u32[]{:S(2)}) %collective-permute-start.1) | collective-permute-done | bytes 16928 | tf_op jit(solution)/shard_map/ppermute | solution.py:30
  70.5 0.1 collective-permute-start.3
  70.5 0.0 collective-permute-done.2.other_sketch
  70.5 0.3 collective-permute-start.5
  70.8 5.6 %sketch_sums.3 = f32[256,128]{1,0:T(8,128)S(1)} custom-call(s32[4224]{0:T(1024)S(1)} %collective-permute-done.1.other_ref, bf16[4096,128]{1,0:T(8,128)(2,1)S(1)} %copy-done, bf16[4096,128]{1,0:T(8,128)(2,1)S(1)} %get-tuple-element.36.right_own, bf16[4096,128]{1,0:T(8,128)(2,1)S(1)} %get-tuple-element.66.sketch_ref, ...), custom_call_target="tpu_custom_call" | custom-call | flops 268435456 | bytes 22000000 | tf_op jit(solution)/shard_map/sketch_sums/pallas_call | solution.py:328
  76.4 0.0 collective-permute-done.3.other_ref
  76.4 31.2 %group_sum_and_factor.3 = (bf16[4096,128]{1,0:T(8,128)(2,1)S(1)}, bf16[256,128]{1,0:T(8,128)(2,1)S(1)}, bf16[256,128]{1,0:T(8,128)(2,1)S(1)}) custom-call(f32[256,128]{1,0:T(8,128)S(1)} %sketch_sums.3, f32[384,128]{1,0:T(8,128)S(1)} %get-tuple-element.38.gram_sums, bf16[4096,256]{1,0:T(8,128)(2,1)S(1)} %get-tuple-element.39.left_cat), custom_call_target="tpu_custom_call" | custom-call | flops 536870912 | bytes 88000000 | tf_op jit(solution)/shard_map/group_sum_and_factor/pallas_call | solution.py:328
  107.6 0.0 collective-permute-done.5.other_ref
  107.7 0.0 collective-permute-done.6.other_sketch
  107.7 0.9 collective-permute-start.9
  108.6 0.0 collective-permute-done.7.right_ref
  108.6 8.2 %right_rows.3.right_ref = bf16[4096,128]{1,0:T(8,128)(2,1)S(1)} custom-call(s32[4096]{0:T(1024)S(1)} %bitcast.29, s32[1,1]{1,0:T(1,128)} %bitcast.12.live_ref, bf16[4096,128]{1,0:T(8,128)(2,1)} %collective-permute-done.7.right_ref, bf16[4096,128]{1,0:T(8,128)(2,1)S(1)} %get-tuple-element.36.right_own, bf16[256,128]{1,0:T(8,128)(2,1)S(1)} %get-tuple-element.45.project_high, ...), custom_call_target="tpu_custom_call" | custom-call | flops 536870912 | bytes 22000000 | tf_op jit(solution)/shard_map/right_rows/pallas_call | solution.py:328
  116.8 0.1 collective-permute-start.8
  116.9 5.2 %own_rows.4 = (bf16[4096,128]{1,0:T(8,128)(2,1)S(1)}, bf16[4096,128]{1,0:T(8,128)(2,1)S(1)}) custom-call(s32[4096]{0:T(1024)S(1)} %bitcast.31, s32[1,1]{1,0:T(1,128)} %bitcast.16.live_ref, bf16[4096,128]{1,0:T(8,128)(2,1)S(1)} %get-tuple-element.47.left_ref, bf16[4096,128]{1,0:T(8,128)(2,1)S(1)} %right_rows.3.right_ref), custom_call_target="tpu_custom_call" | custom-call | flops 524288 | bytes 22000000 | tf_op jit(solution)/shard_map/own_rows/pallas_call | solution.py:328
  122.1 5.3 %sketch_sums.4 = f32[256,128]{1,0:T(8,128)S(1)} custom-call(s32[4224]{0:T(1024)S(1)} %collective-permute-done.5.other_ref, bf16[4096,128]{1,0:T(8,128)(2,1)S(1)} %right_rows.3.right_ref, bf16[4096,128]{1,0:T(8,128)(2,1)S(1)} %get-tuple-element.48.right_own, bf16[4096,128]{1,0:T(8,128)(2,1)S(1)} %get-tuple-element.65.sketch_ref, ...), custom_call_target="tpu_custom_call" | custom-call | flops 268435456 | bytes 22000000 | tf_op jit(solution)/shard_map/sketch_sums/pallas_call | solution.py:328
  127.4 4.9 %collective-permute-done.9.left_ref = bf16[4096,128]{1,0:T(8,128)(2,1)S(1)} collective-permute-done((bf16[4096,128]{1,0:T(8,128)(2,1)S(1)}, bf16[4096,128]{1,0:T(8,128)(2,1)S(1)}, u32[]{:S(2)}, u32[]{:S(2)}) %collective-permute-start.9) | collective-permute-done | bytes 1048608 | tf_op jit(solution)/shard_map/ppermute | solution.py:30
  132.3 6.6 %left_rows.4 = (bf16[4096,256]{1,0:T(8,128)(2,1)S(1)}, f32[384,128]{1,0:T(8,128)S(1)}) custom-call(s32[4096]{0:T(1024)S(1)} %bitcast.25, s32[1,1]{1,0:T(1,128)} %bitcast.16.live_ref, bf16[4096,128]{1,0:T(8,128)(2,1)S(1)} %collective-permute-done.9.left_ref, bf16[4096,128]{1,0:T(8,128)(2,1)S(1)} %get-tuple-element.51.left_own), custom_call_target="tpu_custom_call" | custom-call | flops 536870912 | bytes 22000000 | tf_op jit(solution)/shard_map/left_rows/pallas_call | solution.py:328
  138.9 41.6 %group_sum_and_factor.4 = (bf16[4096,128]{1,0:T(8,128)(2,1)S(1)}, bf16[256,128]{1,0:T(8,128)(2,1)S(1)}, bf16[256,128]{1,0:T(8,128)(2,1)S(1)}) custom-call(f32[256,128]{1,0:T(8,128)S(1)} %sketch_sums.4, f32[384,128]{1,0:T(8,128)S(1)} %get-tuple-element.52.gram_sums, bf16[4096,256]{1,0:T(8,128)(2,1)S(1)} %get-tuple-element.53.left_cat), custom_call_target="tpu_custom_call" | custom-call | flops 536870912 | bytes 88000000 | tf_op jit(solution)/shard_map/group_sum_and_factor/pallas_call | solution.py:328
  180.5 1.8 collective-permute-start.10
  182.3 0.0 collective-permute-done.8.right_ref
  182.3 6.4 %right_rows.4.right_ref = bf16[4096,128]{1,0:T(8,128)(2,1)S(1)} custom-call(s32[4096]{0:T(1024)S(1)} %bitcast.26, s32[1,1]{1,0:T(1,128)} %bitcast.16.live_ref, bf16[4096,128]{1,0:T(8,128)(2,1)S(1)} %collective-permute-done.8.right_ref, bf16[4096,128]{1,0:T(8,128)(2,1)S(1)} %get-tuple-element.48.right_own, ...), custom_call_target="tpu_custom_call" | custom-call | flops 536870912 | bytes 22000000 | tf_op jit(solution)/shard_map/right_rows/pallas_call | solution.py:328
  188.7 1.4 collective-permute-start.11
  190.1 5.5 %own_rows.5 = (bf16[4096,128]{1,0:T(8,128)(2,1)S(1)}, bf16[4096,128]{1,0:T(8,128)(2,1)S(1)}) custom-call(s32[4096]{0:T(1024)S(1)} %bitcast.30, s32[1,1]{1,0:T(1,128)} %bitcast.14.live_ref, bf16[4096,128]{1,0:T(8,128)(2,1)S(1)} %get-tuple-element.56.left_ref, bf16[4096,128]{1,0:T(8,128)(2,1)S(1)} %right_rows.4.right_ref), custom_call_target="tpu_custom_call" | custom-call | flops 524288 | bytes 22000000 | tf_op jit(solution)/shard_map/own_rows/pallas_call | solution.py:328
  195.6 6.5 %sketch_sums.5 = f32[256,128]{1,0:T(8,128)S(1)} custom-call(s32[4224]{0:T(1024)S(1)} %collective-permute-done.3.other_ref, bf16[4096,128]{1,0:T(8,128)(2,1)S(1)} %right_rows.4.right_ref, bf16[4096,128]{1,0:T(8,128)(2,1)S(1)} %get-tuple-element.57.right_own, bf16[4096,128]{1,0:T(8,128)(2,1)S(1)} %get-tuple-element.67.sketch_ref, ...), custom_call_target="tpu_custom_call" | custom-call | flops 268435456 | bytes 22000000 | tf_op jit(solution)/shard_map/sketch_sums/pallas_call | solution.py:328
  202.1 49.1 %collective-permute-done.10.left_ref = bf16[4096,128]{1,0:T(8,128)(2,1)S(1)} collective-permute-done((bf16[4096,128]{1,0:T(8,128)(2,1)S(1)}, bf16[4096,128]{1,0:T(8,128)(2,1)S(1)}, u32[]{:S(2)}, u32[]{:S(2)}) %collective-permute-start.10) | collective-permute-done | bytes 1048608 | tf_op jit(solution)/shard_map/ppermute | solution.py:30
  251.3 6.7 %left_rows.5 = (bf16[4096,256]{1,0:T(8,128)(2,1)S(1)}, f32[384,128]{1,0:T(8,128)S(1)}) custom-call(s32[4096]{0:T(1024)S(1)} %bitcast.22, s32[1,1]{1,0:T(1,128)} %bitcast.14.live_ref, bf16[4096,128]{1,0:T(8,128)(2,1)S(1)} %collective-permute-done.10.left_ref, bf16[4096,128]{1,0:T(8,128)(2,1)S(1)} %get-tuple-element.59.left_own), custom_call_target="tpu_custom_call" | custom-call | flops 536870912 | bytes 22000000 | tf_op jit(solution)/shard_map/left_rows/pallas_call | solution.py:328
  258.0 52.9 %group_sum_and_factor.5 = (bf16[4096,128]{1,0:T(8,128)(2,1)S(1)}, bf16[256,128]{1,0:T(8,128)(2,1)S(1)}, bf16[256,128]{1,0:T(8,128)(2,1)S(1)}) custom-call(f32[256,128]{1,0:T(8,128)S(1)} %sketch_sums.5, f32[384,128]{1,0:T(8,128)S(1)} %get-tuple-element.60.gram_sums, bf16[4096,256]{1,0:T(8,128)(2,1)S(1)} %get-tuple-element.61.left_cat), custom_call_target="tpu_custom_call" | custom-call | flops 536870912 | bytes 88000000 | tf_op jit(solution)/shard_map/group_sum_and_factor/pallas_call | solution.py:328
  310.8 0.0 copy-start.3
  310.8 0.0 copy-start.4
  310.9 7.6 %right_rows.5.right = bf16[4096,128]{1,0:T(8,128)(2,1)} custom-call(s32[4096]{0:T(1024)S(1)} %bitcast.23, s32[1,1]{1,0:T(1,128)} %bitcast.14.live_ref, bf16[4096,128]{1,0:T(8,128)(2,1)S(1)} %collective-permute-done.11.right_ref, bf16[4096,128]{1,0:T(8,128)(2,1)S(1)} %get-tuple-element.57.right_own, bf16[256,128]{1,0:T(8,128)(2,1)S(1)} %get-tuple-element.63.project_high, ...), custom_call_target="tpu_custom_call" | custom-call | flops 536870912 | bytes 22000000 | tf_op jit(solution)/shard_map/right_rows/pallas_call | solution.py:328
  318.5 1.2 copy-done.1
  319.7 8.2 %panel.2 = bf16[4096,128]{1,0:T(8,128)(2,1)S(1)} custom-call(bf16[4096,128]{1,0:T(8,128)(2,1)S(1)} %get-tuple-element.80.left, bf16[4096,128]{1,0:T(8,128)(2,1)S(1)} %copy-done.1, bf16[4096,128]{1,0:T(8,128)(2,1)S(1)} %copy-done.3, bf16[128,128]{1,0:T(8,128)(2,1)S(1)} %copy-done.4), custom_call_target="tpu_custom_call" | custom-call | flops 536870912 | bytes 22000000 | tf_op jit(solution)/shard_map/panel/pallas_call | solution.py:328
  327.9 1.0 copy.19
  328.9 1.0 copy.20
  (17 shorter events, 0.1 us)
Async XLA Ops:
  0.6 7.8 %copy-start.2 = (bf16[4096,128]{1,0:T(8,128)(2,1)S(1)}, bf16[4096,128]{1,0:T(8,128)(2,1)}, u32[]{:S(2)}) copy-start(bf16[4096,128]{1,0:T(8,128)(2,1)} %left_ref.1) | copy-start | bytes 3145732
  0.6 4.0 %copy-start = (bf16[4096,128]{1,0:T(8,128)(2,1)S(1)}, bf16[4096,128]{1,0:T(8,128)(2,1)}, u32[]{:S(2)}) copy-start(bf16[4096,128]{1,0:T(8,128)(2,1)} %right_ref.3) | copy-start | bytes 3145732
  0.7 5.2 %copy-start.5 = (s32[3,4096]{1,0:T(4,128)S(1)}, s32[3,4096]{1,0:T(4,128)}, u32[]{:S(2)}) copy-start(s32[3,4096]{1,0:T(4,128)} %param.12) | copy-start | bytes 147460
  0.7 5.2 %copy-start.7 = (s32[3,1]{0,1:T(1,128)S(1)}, s32[3,1]{0,1:T(1,128)}, u32[]{:S(2)}) copy-start(s32[3,1]{0,1:T(1,128)} %param.13) | copy-start | bytes 40
  0.7 7.8 %copy-start.6 = (s32[3,4096]{1,0:T(4,128)S(1)}, s32[3,4096]{1,0:T(4,128)}, u32[]{:S(2)}) copy-start(s32[3,4096]{1,0:T(4,128)} %param.11) | copy-start | bytes 147460
  0.7 24.3 %collective-permute-start = (bf16[4096,128]{1,0:T(8,128)(2,1)}, bf16[4096,128]{1,0:T(8,128)(2,1)S(1)}, u32[]{:S(2)}, u32[]{:S(2)}) collective-permute-start(bf16[4096,128]{1,0:T(8,128)(2,1)} %left_ref.1), channel_id=1, source_target_pairs={{0,4},{4,0},{8,12},{12,8},{16,20},{20,16},{24,28},{28,24},{1,5},{5... | collective-permute-start | bytes 3145736 | tf_op jit(solution)/shard_map/ppermute | solution.py:30
  4.0 66.5 %collective-permute-start.2 = (bf16[4096,128]{1,0:T(8,128)(2,1)S(1)}, bf16[4096,128]{1,0:T(8,128)(2,1)S(1)}, u32[]{:S(2)}, u32[]{:S(2)}) collective-permute-start(bf16[4096,128]{1,0:T(8,128)(2,1)S(1)} %get-tuple-element.66.sketch_ref), channel_id=1, source_target_pairs={{0,4},{4,0},{8,12},{12,8},{16,20},{20,16},{24,28},{28,24},{1,5},{5... | collective-permute-start | bytes 3145736 | tf_op jit(solution)/shard_map/ppermute | solution.py:30
  4.5 72.0 %collective-permute-start.4 = (bf16[4096,128]{1,0:T(8,128)(2,1)S(1)}, bf16[4096,128]{1,0:T(8,128)(2,1)S(1)}, u32[]{:S(2)}, u32[]{:S(2)}) collective-permute-start(bf16[4096,128]{1,0:T(8,128)(2,1)S(1)} %get-tuple-element.67.sketch_ref), channel_id=1, source_target_pairs={{0,16},{16,0},{4,20},{20,4},{8,24},{24,8},{12,28},{28,12},{1,17},{... | collective-permute-start | bytes 3145736 | tf_op jit(solution)/shard_map/ppermute | solution.py:30
  4.5 103.1 %collective-permute-start.6 = (bf16[4096,128]{1,0:T(8,128)(2,1)S(1)}, bf16[4096,128]{1,0:T(8,128)(2,1)S(1)}, u32[]{:S(2)}, u32[]{:S(2)}) collective-permute-start(bf16[4096,128]{1,0:T(8,128)(2,1)S(1)} %get-tuple-element.65.sketch_ref), channel_id=1, source_target_pairs={{0,8},{8,0},{4,12},{12,4},{16,24},{24,16},{20,28},{28,20},{1,9},{9... | collective-permute-start | bytes 3145736 | tf_op jit(solution)/shard_map/ppermute | solution.py:30
  4.6 103.9 %collective-permute-start.7 = (bf16[4096,128]{1,0:T(8,128)(2,1)S(1)}, bf16[4096,128]{1,0:T(8,128)(2,1)}, u32[]{:S(2)}, u32[]{:S(2)}) collective-permute-start(bf16[4096,128]{1,0:T(8,128)(2,1)S(1)} %copy-done), channel_id=1, source_target_pairs={{0,4},{4,0},{8,12},{12,8},{16,20},{20,16},{24,28},{28,24},{1,5},{5... | collective-permute-start | bytes 3145736 | tf_op jit(solution)/shard_map/ppermute | solution.py:30
  25.0 45.5 %collective-permute-start.1 = (s32[4224]{0:T(1024)S(1)}, s32[4224]{0:T(1024)S(1)}, u32[]{:S(2)}, u32[]{:S(2)}) collective-permute-start(s32[4224]{0:T(1024)S(1)} %concatenate.9), channel_id=1, source_target_pairs={{0,4},{4,0},{8,12},{12,8},{16,20},{20,16},{24,28},{28,24},{1,5},{5... | collective-permute-start | bytes 50696 | tf_op jit(solution)/shard_map/ppermute | solution.py:30
  70.5 5.9 %collective-permute-start.3 = (s32[4224]{0:T(1024)S(1)}, s32[4224]{0:T(1024)S(1)}, u32[]{:S(2)}, u32[]{:S(2)}) collective-permute-start(s32[4224]{0:T(1024)S(1)} %concatenate.10), channel_id=1, source_target_pairs={{0,16},{16,0},{4,20},{20,4},{8,24},{24,8},{12,28},{28,12},{1,17},{... | collective-permute-start | bytes 50696 | tf_op jit(solution)/shard_map/ppermute | solution.py:30
  70.5 37.1 %collective-permute-start.5 = (s32[4224]{0:T(1024)S(1)}, s32[4224]{0:T(1024)S(1)}, u32[]{:S(2)}, u32[]{:S(2)}) collective-permute-start(s32[4224]{0:T(1024)S(1)} %concatenate.11), channel_id=1, source_target_pairs={{0,8},{8,0},{4,12},{12,4},{16,24},{24,16},{20,28},{28,20},{1,9},{9... | collective-permute-start | bytes 50696 | tf_op jit(solution)/shard_map/ppermute | solution.py:30
  107.7 24.6 %collective-permute-start.9 = (bf16[4096,128]{1,0:T(8,128)(2,1)S(1)}, bf16[4096,128]{1,0:T(8,128)(2,1)S(1)}, u32[]{:S(2)}, u32[]{:S(2)}) collective-permute-start(bf16[4096,128]{1,0:T(8,128)(2,1)S(1)} %get-tuple-element.47.left_ref), channel_id=1, source_target_pairs={{0,8},{8,0},{4,12},{12,4},{16,24},{24,16},{20,28},{28,20},{1,9},{9... | collective-permute-start | bytes 3145736 | tf_op jit(solution)/shard_map/ppermute | solution.py:30
  116.8 65.5 %collective-permute-start.8 = (bf16[4096,128]{1,0:T(8,128)(2,1)S(1)}, bf16[4096,128]{1,0:T(8,128)(2,1)S(1)}, u32[]{:S(2)}, u32[]{:S(2)}) collective-permute-start(bf16[4096,128]{1,0:T(8,128)(2,1)S(1)} %right_rows.3.right_ref), channel_id=1, source_target_pairs={{0,8},{8,0},{4,12},{12,4},{16,24},{24,16},{20,28},{28,20},{1,9},{9... | collective-permute-start | bytes 3145736 | tf_op jit(solution)/shard_map/ppermute | solution.py:30
  180.5 70.7 %collective-permute-start.10 = (bf16[4096,128]{1,0:T(8,128)(2,1)S(1)}, bf16[4096,128]{1,0:T(8,128)(2,1)S(1)}, u32[]{:S(2)}, u32[]{:S(2)}) collective-permute-start(bf16[4096,128]{1,0:T(8,128)(2,1)S(1)} %get-tuple-element.56.left_ref), channel_id=1, source_target_pairs={{0,16},{16,0},{4,20},{20,4},{8,24},{24,8},{12,28},{28,12},{1,17},{... | collective-permute-start | bytes 3145736 | tf_op jit(solution)/shard_map/ppermute | solution.py:30
  188.7 122.2 %collective-permute-start.11 = (bf16[4096,128]{1,0:T(8,128)(2,1)S(1)}, bf16[4096,128]{1,0:T(8,128)(2,1)S(1)}, u32[]{:S(2)}, u32[]{:S(2)}) collective-permute-start(bf16[4096,128]{1,0:T(8,128)(2,1)S(1)} %right_rows.4.right_ref), channel_id=1, source_target_pairs={{0,16},{16,0},{4,20},{20,4},{8,24},{24,8},{12,28},{28,12},{1,17},{... | collective-permute-start | bytes 3145736 | tf_op jit(solution)/shard_map/ppermute | solution.py:30
  310.8 7.7 %copy-start.3 = (bf16[4096,128]{1,0:T(8,128)(2,1)S(1)}, bf16[4096,128]{1,0:T(8,128)(2,1)}, u32[]{:S(2)}) copy-start(bf16[4096,128]{1,0:T(8,128)(2,1)} %panel.3) | copy-start | bytes 3145732
  310.8 7.7 %copy-start.4 = (bf16[128,128]{1,0:T(8,128)(2,1)S(1)}, bf16[128,128]{1,0:T(8,128)(2,1)}, u32[]{:S(2)}) copy-start(bf16[128,128]{1,0:T(8,128)(2,1)} %inverse.1) | copy-start | bytes 98308
  318.5 1.2 copy-start.1

commit v3 on v2

--- a/solution.py
+++ b/solution.py
@@ -359,7 +359,14 @@
         live = live_rows[level].reshape(1, 1)
         if level:
             left_sibling = from_partner(left, "leaf", level)
-        right_sibling = from_partner(right, "leaf", level)
+        if level == 0:
+            ahead = (others[0], other_sketch[0])
+            right_sent, (others[0], other_sketch[0]) = lax.optimization_barrier((right, ahead))
+        elif level == level_count - 1:
+            right_sent, left_sibling = lax.optimization_barrier((right, left_sibling))
+        else:
+            right_sent = right
+        right_sibling = from_partner(right_sent, "leaf", level)
         with jax.named_scope("own_rows"):
             left_own, right_own = call(
                 own_kernel, (narrow, narrow), [map_own[level], live, left, right], 2, pairs,

time: 331 us -> 323 us (0.976)
  waiting for transfers between devices: 99.9 us -> 79.2 us
  Pallas kernels: 212 us -> 226 us
    ppermute x12, waiting for transfers between devices: 99.9 us -> 79.2 us  [from_partner(): return lax.ppermute(block, axis, route)]
    pallas_call x16, Pallas kernels: 212 us -> 226 us  [call(): pl.pallas_call(kernel, out_shape=outs, in_specs=[SMEM_SPEC] * scalars + [...]
  transfers between devices with their start and end apart: 12 -> 12, of which waited for: 4 -> 3; matrix products, arithmetic and copies ran while one was open for 1% -> 1% of each run, Pallas kernels for 60% -> 65%
where the time goes in v3:
time: 323 us; the launch traced here: 322 us
  Pallas kernels  226 us (70%)
  waiting for transfers between devices  79.2 us (25%)
  starting transfers between devices  8.4 us (3%)
  local copies, waits for them, and re-layouts  7.87 us (2%)
    pallas_call x16, Pallas kernels, call(): pl.pallas_call(kernel, out_shape=outs, in_specs=[SMEM_SPEC] * scalars + [...  226 us
    ppermute x12, waiting for transfers between devices, from_partner(): return lax.ppermute(block, axis, route)  79.2 us
    ppermute x12, starting transfers between devices, from_partner(): return lax.ppermute(block, axis, route)  8.4 us
  transfers between devices with their start and end apart: 12, of which 3 were waited for; matrix products, arithmetic and copies ran while one was open for 1% of the time, Pallas kernels for 65%

profile of v3, /device:TPU:25, one launch (start us, length us, event | category | flops | bytes accessed | tf_op | source)
XLA Modules:
  0.0 321.9 jit_solution(17394626802542029073)
XLA Ops:
  0.7 1.3 collective-permute-start
  2.0 2.1 slice_bitcast_fusion
  4.0 0.5 collective-permute-start.2
  4.5 0.1 collective-permute-start.4
  4.6 0.1 collective-permute-start.6
  4.8 0.6 fusion.2
  5.4 0.6 concatenate.9
  6.0 1.2 collective-permute-start.1
  7.2 0.7 concatenate.10
  7.9 0.7 concatenate.11
  8.5 6.2 %own_rows.3 = (bf16[4096,128]{1,0:T(8,128)(2,1)S(1)}, bf16[4096,128]{1,0:T(8,128)(2,1)S(1)}) custom-call(s32[4096]{0:T(1024)S(1)} %bitcast.32, s32[1,1]{1,0:T(1,128)} %bitcast.12.live_ref, bf16[4096,128]{1,0:T(8,128)(2,1)S(1)} %copy-done.2, bf16[4096,128]{1,0:T(8,128)(2,1)S(1)} %copy-done), custom_call_target="tpu_custom_call" | custom-call | flops 524288 | bytes 22000000 | tf_op jit(solution)/shard_map/own_rows/pallas_call | solution.py:328
  14.8 33.1 %collective-permute-done.1.other_ref = s32[4224]{0:T(1024)S(1)} collective-permute-done((s32[4224]{0:T(1024)S(1)}, s32[4224]{0:T(1024)S(1)}, u32[]{:S(2)}, u32[]{:S(2)}) %collective-permute-start.1) | collective-permute-done | bytes 16928 | tf_op jit(solution)/shard_map/ppermute | solution.py:30
  47.9 0.1 collective-permute-start.3
  48.0 0.0 collective-permute-done.2.other_sketch
  48.0 0.3 collective-permute-start.5
  48.2 0.0 collective-permute-done.left_ref
  48.2 1.1 collective-permute-start.7
  49.4 7.2 %left_rows.3 = (bf16[4096,256]{1,0:T(8,128)(2,1)S(1)}, f32[384,128]{1,0:T(8,128)S(1)}) custom-call(s32[4096]{0:T(1024)S(1)} %bitcast.28, s32[1,1]{1,0:T(1,128)} %bitcast.12.live_ref, bf16[4096,128]{1,0:T(8,128)(2,1)S(1)} %collective-permute-done.left_ref, bf16[4096,128]{1,0:T(8,128)(2,1)S(1)} %get-tuple-element.39.left_own), custom_call_target="tpu_custom_call" | custom-call | flops 536870912 | bytes 22000000 | tf_op jit(solution)/shard_map/left_rows/pallas_call | solution.py:328
  56.6 6.2 %sketch_sums.3 = f32[256,128]{1,0:T(8,128)S(1)} custom-call(s32[4224]{0:T(1024)S(1)} %collective-permute-done.1.other_ref, bf16[4096,128]{1,0:T(8,128)(2,1)S(1)} %copy-done, bf16[4096,128]{1,0:T(8,128)(2,1)S(1)} %get-tuple-element.42.right_own, bf16[4096,128]{1,0:T(8,128)(2,1)S(1)} %get-tuple-element.76.sketch_ref, ...), custom_call_target="tpu_custom_call" | custom-call | flops 268435456 | bytes 22000000 | tf_op jit(solution)/shard_map/sketch_sums/pallas_call | solution.py:328
  62.8 0.0 collective-permute-done.3.other_ref
  62.8 0.0 collective-permute-done.4.other_sketch
  62.9 34.8 %group_sum_and_factor.3 = (bf16[4096,128]{1,0:T(8,128)(2,1)S(1)}, bf16[256,128]{1,0:T(8,128)(2,1)S(1)}, bf16[256,128]{1,0:T(8,128)(2,1)S(1)}) custom-call(f32[256,128]{1,0:T(8,128)S(1)} %sketch_sums.3, f32[384,128]{1,0:T(8,128)S(1)} %get-tuple-element.45.gram_sums, bf16[4096,256]{1,0:T(8,128)(2,1)S(1)} %get-tuple-element.46.left_cat), custom_call_target="tpu_custom_call" | custom-call | flops 536870912 | bytes 88000000 | tf_op jit(solution)/shard_map/group_sum_and_factor/pallas_call | solution.py:328
  97.7 0.0 collective-permute-done.5.other_ref
  97.7 0.0 collective-permute-done.6.other_sketch
  97.7 1.4 collective-permute-start.9
  99.1 0.0 collective-permute-done.7.right_ref
  99.1 7.6 %right_rows.3.right_ref = bf16[4096,128]{1,0:T(8,128)(2,1)S(1)} custom-call(s32[4096]{0:T(1024)S(1)} %bitcast.29, s32[1,1]{1,0:T(1,128)} %bitcast.12.live_ref, bf16[4096,128]{1,0:T(8,128)(2,1)} %collective-permute-done.7.right_ref, bf16[4096,128]{1,0:T(8,128)(2,1)S(1)} %get-tuple-element.42.right_own, bf16[256,128]{1,0:T(8,128)(2,1)S(1)} %get-tuple-element.53.project_high, ...), custom_call_target="tpu_custom_call" | custom-call | flops 536870912 | bytes 22000000 | tf_op jit(solution)/shard_map/right_rows/pallas_call | solution.py:328
  106.7 0.1 collective-permute-start.8
  106.7 4.8 %own_rows.4 = (bf16[4096,128]{1,0:T(8,128)(2,1)S(1)}, bf16[4096,128]{1,0:T(8,128)(2,1)S(1)}) custom-call(s32[4096]{0:T(1024)S(1)} %bitcast.31, s32[1,1]{1,0:T(1,128)} %bitcast.16.live_ref, bf16[4096,128]{1,0:T(8,128)(2,1)S(1)} %get-tuple-element.55.left_ref, bf16[4096,128]{1,0:T(8,128)(2,1)S(1)} %right_rows.3.right_ref), custom_call_target="tpu_custom_call" | custom-call | flops 524288 | bytes 22000000 | tf_op jit(solution)/shard_map/own_rows/pallas_call | solution.py:328
  111.5 4.3 %sketch_sums.4 = f32[256,128]{1,0:T(8,128)S(1)} custom-call(s32[4224]{0:T(1024)S(1)} %collective-permute-done.5.other_ref, bf16[4096,128]{1,0:T(8,128)(2,1)S(1)} %right_rows.3.right_ref, bf16[4096,128]{1,0:T(8,128)(2,1)S(1)} %get-tuple-element.56.right_own, bf16[4096,128]{1,0:T(8,128)(2,1)S(1)} %get-tuple-element.75.sketch_ref, ...), custom_call_target="tpu_custom_call" | custom-call | flops 268435456 | bytes 22000000 | tf_op jit(solution)/shard_map/sketch_sums/pallas_call | solution.py:328
  115.9 6.5 %collective-permute-done.9.left_ref = bf16[4096,128]{1,0:T(8,128)(2,1)S(1)} collective-permute-done((bf16[4096,128]{1,0:T(8,128)(2,1)S(1)}, bf16[4096,128]{1,0:T(8,128)(2,1)S(1)}, u32[]{:S(2)}, u32[]{:S(2)}) %collective-permute-start.9) | collective-permute-done | bytes 1048608 | tf_op jit(solution)/shard_map/ppermute | solution.py:30
  122.4 6.3 %left_rows.4 = (bf16[4096,256]{1,0:T(8,128)(2,1)S(1)}, f32[384,128]{1,0:T(8,128)S(1)}) custom-call(s32[4096]{0:T(1024)S(1)} %bitcast.25, s32[1,1]{1,0:T(1,128)} %bitcast.16.live_ref, bf16[4096,128]{1,0:T(8,128)(2,1)S(1)} %collective-permute-done.9.left_ref, bf16[4096,128]{1,0:T(8,128)(2,1)S(1)} %get-tuple-element.59.left_own), custom_call_target="tpu_custom_call" | custom-call | flops 536870912 | bytes 22000000 | tf_op jit(solution)/shard_map/left_rows/pallas_call | solution.py:328
  128.6 42.2 %group_sum_and_factor.4 = (bf16[4096,128]{1,0:T(8,128)(2,1)S(1)}, bf16[256,128]{1,0:T(8,128)(2,1)S(1)}, bf16[256,128]{1,0:T(8,128)(2,1)S(1)}) custom-call(f32[256,128]{1,0:T(8,128)S(1)} %sketch_sums.4, f32[384,128]{1,0:T(8,128)S(1)} %get-tuple-element.60.gram_sums, bf16[4096,256]{1,0:T(8,128)(2,1)S(1)} %get-tuple-element.61.left_cat), custom_call_target="tpu_custom_call" | custom-call | flops 536870912 | bytes 88000000 | tf_op jit(solution)/shard_map/group_sum_and_factor/pallas_call | solution.py:328
  170.9 2.4 collective-permute-start.10
  173.3 6.0 %right_rows.4.right_ref = bf16[4096,128]{1,0:T(8,128)(2,1)S(1)} custom-call(s32[4096]{0:T(1024)S(1)} %bitcast.26, s32[1,1]{1,0:T(1,128)} %bitcast.16.live_ref, bf16[4096,128]{1,0:T(8,128)(2,1)S(1)} %collective-permute-done.8.right_ref, bf16[4096,128]{1,0:T(8,128)(2,1)S(1)} %get-tuple-element.56.right_own, ...), custom_call_target="tpu_custom_call" | custom-call | flops 536870912 | bytes 22000000 | tf_op jit(solution)/shard_map/right_rows/pallas_call | solution.py:328
  179.3 39.5 %collective-permute-done.10.left_ref = bf16[4096,128]{1,0:T(8,128)(2,1)S(1)} collective-permute-done((bf16[4096,128]{1,0:T(8,128)(2,1)S(1)}, bf16[4096,128]{1,0:T(8,128)(2,1)S(1)}, u32[]{:S(2)}, u32[]{:S(2)}) %collective-permute-start.10) | collective-permute-done | bytes 1048608 | tf_op jit(solution)/shard_map/ppermute | solution.py:30
  218.8 0.0 collective-permute-start.11
  218.8 6.6 %own_rows.5 = (bf16[4096,128]{1,0:T(8,128)(2,1)S(1)}, bf16[4096,128]{1,0:T(8,128)(2,1)S(1)}) custom-call(s32[4096]{0:T(1024)S(1)} %bitcast.30, s32[1,1]{1,0:T(1,128)} %bitcast.14.live_ref, bf16[4096,128]{1,0:T(8,128)(2,1)S(1)} %get-tuple-element.64.left_ref, bf16[4096,128]{1,0:T(8,128)(2,1)S(1)} %right_rows.4.right_ref), custom_call_target="tpu_custom_call" | custom-call | flops 524288 | bytes 22000000 | tf_op jit(solution)/shard_map/own_rows/pallas_call | solution.py:328
  225.4 4.1 %sketch_sums.5 = f32[256,128]{1,0:T(8,128)S(1)} custom-call(s32[4224]{0:T(1024)S(1)} %collective-permute-done.3.other_ref, bf16[4096,128]{1,0:T(8,128)(2,1)S(1)} %right_rows.4.right_ref, bf16[4096,128]{1,0:T(8,128)(2,1)S(1)} %get-tuple-element.65.right_own, bf16[4096,128]{1,0:T(8,128)(2,1)S(1)} %get-tuple-element.77.sketch_ref, ...), custom_call_target="tpu_custom_call" | custom-call | flops 268435456 | bytes 22000000 | tf_op jit(solution)/shard_map/sketch_sums/pallas_call | solution.py:328
  229.6 7.5 %left_rows.5 = (bf16[4096,256]{1,0:T(8,128)(2,1)S(1)}, f32[384,128]{1,0:T(8,128)S(1)}) custom-call(s32[4096]{0:T(1024)S(1)} %bitcast.22, s32[1,1]{1,0:T(1,128)} %bitcast.14.live_ref, bf16[4096,128]{1,0:T(8,128)(2,1)S(1)} %collective-permute-done.10.left_ref, bf16[4096,128]{1,0:T(8,128)(2,1)S(1)} %get-tuple-element.68.left_own), custom_call_target="tpu_custom_call" | custom-call | flops 536870912 | bytes 22000000 | tf_op jit(solution)/shard_map/left_rows/pallas_call | solution.py:328
  237.1 65.8 %group_sum_and_factor.5 = (bf16[4096,128]{1,0:T(8,128)(2,1)S(1)}, bf16[256,128]{1,0:T(8,128)(2,1)S(1)}, bf16[256,128]{1,0:T(8,128)(2,1)S(1)}) custom-call(f32[256,128]{1,0:T(8,128)S(1)} %sketch_sums.5, f32[384,128]{1,0:T(8,128)S(1)} %get-tuple-element.69.gram_sums, bf16[4096,256]{1,0:T(8,128)(2,1)S(1)} %get-tuple-element.70.left_cat), custom_call_target="tpu_custom_call" | custom-call | flops 536870912 | bytes 88000000 | tf_op jit(solution)/shard_map/group_sum_and_factor/pallas_call | solution.py:328
  303.0 0.0 copy-start.3
  303.0 0.0 copy-start.4
  303.0 8.5 %right_rows.5.right = bf16[4096,128]{1,0:T(8,128)(2,1)} custom-call(s32[4096]{0:T(1024)S(1)} %bitcast.23, s32[1,1]{1,0:T(1,128)} %bitcast.14.live_ref, bf16[4096,128]{1,0:T(8,128)(2,1)S(1)} %collective-permute-done.11.right_ref, bf16[4096,128]{1,0:T(8,128)(2,1)S(1)} %get-tuple-element.65.right_own, bf16[256,128]{1,0:T(8,128)(2,1)S(1)} %get-tuple-element.73.project_high, ...), custom_call_target="tpu_custom_call" | custom-call | flops 536870912 | bytes 22000000 | tf_op jit(solution)/shard_map/right_rows/pallas_call | solution.py:328
  311.5 1.2 copy-done.1
  312.7 7.2 %panel.2 = bf16[4096,128]{1,0:T(8,128)(2,1)S(1)} custom-call(bf16[4096,128]{1,0:T(8,128)(2,1)S(1)} %get-tuple-element.90.left, bf16[4096,128]{1,0:T(8,128)(2,1)S(1)} %copy-done.1, bf16[4096,128]{1,0:T(8,128)(2,1)S(1)} %copy-done.3, bf16[128,128]{1,0:T(8,128)(2,1)S(1)} %copy-done.4), custom_call_target="tpu_custom_call" | custom-call | flops 536870912 | bytes 22000000 | tf_op jit(solution)/shard_map/panel/pallas_call | solution.py:328
  320.0 1.0 copy.19
  321.0 1.0 copy.20
  (17 shorter events, 0.1 us)
Async XLA Ops:
  0.6 7.9 %copy-start.2 = (bf16[4096,128]{1,0:T(8,128)(2,1)S(1)}, bf16[4096,128]{1,0:T(8,128)(2,1)}, u32[]{:S(2)}) copy-start(bf16[4096,128]{1,0:T(8,128)(2,1)} %left_ref.1) | copy-start | bytes 3145732
  0.6 4.1 %copy-start.5 = (s32[3,4096]{1,0:T(4,128)S(1)}, s32[3,4096]{1,0:T(4,128)}, u32[]{:S(2)}) copy-start(s32[3,4096]{1,0:T(4,128)} %param.12) | copy-start | bytes 147460
  0.7 4.1 %copy-start.7 = (s32[3,1]{0,1:T(1,128)S(1)}, s32[3,1]{0,1:T(1,128)}, u32[]{:S(2)}) copy-start(s32[3,1]{0,1:T(1,128)} %param.13) | copy-start | bytes 40
  0.7 6.5 %copy-start.6 = (s32[3,4096]{1,0:T(4,128)S(1)}, s32[3,4096]{1,0:T(4,128)}, u32[]{:S(2)}) copy-start(s32[3,4096]{1,0:T(4,128)} %param.11) | copy-start | bytes 147460
  0.7 7.9 %copy-start = (bf16[4096,128]{1,0:T(8,128)(2,1)S(1)}, bf16[4096,128]{1,0:T(8,128)(2,1)}, u32[]{:S(2)}) copy-start(bf16[4096,128]{1,0:T(8,128)(2,1)} %right_ref.3) | copy-start | bytes 3145732
  0.7 47.5 %collective-permute-start = (bf16[4096,128]{1,0:T(8,128)(2,1)}, bf16[4096,128]{1,0:T(8,128)(2,1)S(1)}, u32[]{:S(2)}, u32[]{:S(2)}) collective-permute-start(bf16[4096,128]{1,0:T(8,128)(2,1)} %left_ref.1), channel_id=1, source_target_pairs={{0,4},{4,0},{8,12},{12,8},{16,20},{20,16},{24,28},{28,24},{1,5},{5... | collective-permute-start | bytes 3145736 | tf_op jit(solution)/shard_map/ppermute | solution.py:30
  4.0 43.9 %collective-permute-start.2 = (bf16[4096,128]{1,0:T(8,128)(2,1)S(1)}, bf16[4096,128]{1,0:T(8,128)(2,1)S(1)}, u32[]{:S(2)}, u32[]{:S(2)}) collective-permute-start(bf16[4096,128]{1,0:T(8,128)(2,1)S(1)} %get-tuple-element.76.sketch_ref), channel_id=1, source_target_pairs={{0,4},{4,0},{8,12},{12,8},{16,20},{20,16},{24,28},{28,24},{1,5},{5... | collective-permute-start | bytes 3145736 | tf_op jit(solution)/shard_map/ppermute | solution.py:30
  4.5 58.3 %collective-permute-start.4 = (bf16[4096,128]{1,0:T(8,128)(2,1)S(1)}, bf16[4096,128]{1,0:T(8,128)(2,1)S(1)}, u32[]{:S(2)}, u32[]{:S(2)}) collective-permute-start(bf16[4096,128]{1,0:T(8,128)(2,1)S(1)} %get-tuple-element.77.sketch_ref), channel_id=1, source_target_pairs={{0,16},{16,0},{4,20},{20,4},{8,24},{24,8},{12,28},{28,12},{1,17},{... | collective-permute-start | bytes 3145736 | tf_op jit(solution)/shard_map/ppermute | solution.py:30
  4.6 93.1 %collective-permute-start.6 = (bf16[4096,128]{1,0:T(8,128)(2,1)S(1)}, bf16[4096,128]{1,0:T(8,128)(2,1)S(1)}, u32[]{:S(2)}, u32[]{:S(2)}) collective-permute-start(bf16[4096,128]{1,0:T(8,128)(2,1)S(1)} %get-tuple-element.75.sketch_ref), channel_id=1, source_target_pairs={{0,8},{8,0},{4,12},{12,4},{16,24},{24,16},{20,28},{28,20},{1,9},{9... | collective-permute-start | bytes 3145736 | tf_op jit(solution)/shard_map/ppermute | solution.py:30
  6.0 41.9 %collective-permute-start.1 = (s32[4224]{0:T(1024)S(1)}, s32[4224]{0:T(1024)S(1)}, u32[]{:S(2)}, u32[]{:S(2)}) collective-permute-start(s32[4224]{0:T(1024)S(1)} %concatenate.9), channel_id=1, source_target_pairs={{0,4},{4,0},{8,12},{12,8},{16,20},{20,16},{24,28},{28,24},{1,5},{5... | collective-permute-start | bytes 50696 | tf_op jit(solution)/shard_map/ppermute | solution.py:30
  47.9 14.9 %collective-permute-start.3 = (s32[4224]{0:T(1024)S(1)}, s32[4224]{0:T(1024)S(1)}, u32[]{:S(2)}, u32[]{:S(2)}) collective-permute-start(s32[4224]{0:T(1024)S(1)} %concatenate.10), channel_id=1, source_target_pairs={{0,16},{16,0},{4,20},{20,4},{8,24},{24,8},{12,28},{28,12},{1,17},{... | collective-permute-start | bytes 50696 | tf_op jit(solution)/shard_map/ppermute | solution.py:30
  48.0 49.7 %collective-permute-start.5 = (s32[4224]{0:T(1024)S(1)}, s32[4224]{0:T(1024)S(1)}, u32[]{:S(2)}, u32[]{:S(2)}) collective-permute-start(s32[4224]{0:T(1024)S(1)} %concatenate.11), channel_id=1, source_target_pairs={{0,8},{8,0},{4,12},{12,4},{16,24},{24,16},{20,28},{28,20},{1,9},{9... | collective-permute-start | bytes 50696 | tf_op jit(solution)/shard_map/ppermute | solution.py:30
  48.2 50.8 %collective-permute-start.7 = (bf16[4096,128]{1,0:T(8,128)(2,1)S(1)}, bf16[4096,128]{1,0:T(8,128)(2,1)}, u32[]{:S(2)}, u32[]{:S(2)}) collective-permute-start(bf16[4096,128]{1,0:T(8,128)(2,1)S(1)} %copy-done), channel_id=1, source_target_pairs={{0,4},{4,0},{8,12},{12,8},{16,20},{20,16},{24,28},{28,24},{1,5},{5... | collective-permute-start | bytes 3145736 | tf_op jit(solution)/shard_map/ppermute | solution.py:30
  97.7 24.7 %collective-permute-start.9 = (bf16[4096,128]{1,0:T(8,128)(2,1)S(1)}, bf16[4096,128]{1,0:T(8,128)(2,1)S(1)}, u32[]{:S(2)}, u32[]{:S(2)}) collective-permute-start(bf16[4096,128]{1,0:T(8,128)(2,1)S(1)} %get-tuple-element.55.left_ref), channel_id=1, source_target_pairs={{0,8},{8,0},{4,12},{12,4},{16,24},{24,16},{20,28},{28,20},{1,9},{9... | collective-permute-start | bytes 3145736 | tf_op jit(solution)/shard_map/ppermute | solution.py:30
  106.7 66.6 %collective-permute-start.8 = (bf16[4096,128]{1,0:T(8,128)(2,1)S(1)}, bf16[4096,128]{1,0:T(8,128)(2,1)S(1)}, u32[]{:S(2)}, u32[]{:S(2)}) collective-permute-start(bf16[4096,128]{1,0:T(8,128)(2,1)S(1)} %right_rows.3.right_ref), channel_id=1, source_target_pairs={{0,8},{8,0},{4,12},{12,4},{16,24},{24,16},{20,28},{28,20},{1,9},{9... | collective-permute-start | bytes 3145736 | tf_op jit(solution)/shard_map/ppermute | solution.py:30
  170.9 47.9 %collective-permute-start.10 = (bf16[4096,128]{1,0:T(8,128)(2,1)S(1)}, bf16[4096,128]{1,0:T(8,128)(2,1)S(1)}, u32[]{:S(2)}, u32[]{:S(2)}) collective-permute-start(bf16[4096,128]{1,0:T(8,128)(2,1)S(1)} %get-tuple-element.64.left_ref), channel_id=1, source_target_pairs={{0,16},{16,0},{4,20},{20,4},{8,24},{24,8},{12,28},{28,12},{1,17},{... | collective-permute-start | bytes 3145736 | tf_op jit(solution)/shard_map/ppermute | solution.py:30
  218.8 84.1 %collective-permute-start.11 = (bf16[4096,128]{1,0:T(8,128)(2,1)S(1)}, bf16[4096,128]{1,0:T(8,128)(2,1)S(1)}, u32[]{:S(2)}, u32[]{:S(2)}) collective-permute-start(bf16[4096,128]{1,0:T(8,128)(2,1)S(1)} %right_rows.4.right_ref), channel_id=1, source_target_pairs={{0,16},{16,0},{4,20},{20,4},{8,24},{24,8},{12,28},{28,12},{1,17},{... | collective-permute-start | bytes 3145736 | tf_op jit(solution)/shard_map/ppermute | solution.py:30
  303.0 8.6 %copy-start.3 = (bf16[4096,128]{1,0:T(8,128)(2,1)S(1)}, bf16[4096,128]{1,0:T(8,128)(2,1)}, u32[]{:S(2)}) copy-start(bf16[4096,128]{1,0:T(8,128)(2,1)} %panel.3) | copy-start | bytes 3145732
  303.0 8.5 %copy-start.4 = (bf16[128,128]{1,0:T(8,128)(2,1)S(1)}, bf16[128,128]{1,0:T(8,128)(2,1)}, u32[]{:S(2)}) copy-start(bf16[128,128]{1,0:T(8,128)(2,1)} %inverse.1) | copy-start | bytes 98308
  311.5 1.2 copy-start.1
